TPU v7x, 128 devices: a whole 4x4x4 slice. The times are simulated.
128 devices in a mesh: dp: 64 (over x, y_hi, z, core), tensor: 2 (over y_lo).
Axes of the slice: x: 4, y: 4 (y_hi: 2, y_lo: 2; y = y_hi * 2 + y_lo), z: 4, core: 2. Of those that a mesh axis runs over, the one named last changes fastest.
Arguments:
- tokens: bfloat16 [16384, 1024], P('dp'), may hold values from -16 to 16
- segments: int32 [64, 256], P('dp'), may hold values from 0 to 3, never falling along the last dimension, each value on 1 to 128 neighbouring positions
- routes: int32 [2, 16384, 2], P(None, 'dp'), may hold values from 0 to 3, all different within a row
- norm_attention: bfloat16 [2, 1024], replicated, may hold values from 0.099609375 to 1.8984375
- query_weight: bfloat16 [2, 1024, 1024], P(None, None, 'tensor'), may hold values from -0.1875 to 0.1875
- key_matrix: bfloat16 [2, 1024, 512], P(None, None, 'tensor'), may hold values from -0.1875 to 0.1875
- value_matrix: bfloat16 [2, 1024, 512], P(None, None, 'tensor'), may hold values from -0.1875 to 0.1875
- output_weight: bfloat16 [2, 1024, 1024], P(None, 'tensor'), may hold values from -0.75 to 0.75
- norm_experts: bfloat16 [2, 1024], replicated, may hold values from 0.099609375 to 1.8984375
- router_weight: bfloat16 [2, 1024, 4], replicated, may hold values from -0.109375 to 0.109375
- gate_weight: bfloat16 [2, 4, 1024, 512], P(None, None, None, 'tensor'), may hold values from -0.1875 to 0.1875
- up_weight: bfloat16 [2, 4, 1024, 512], P(None, None, None, 'tensor'), may hold values from -0.1875 to 0.1875
- down_weight: bfloat16 [2, 4, 512, 1024], P(None, None, 'tensor'), may hold values from -0.375 to 0.375
- cotangent: bfloat16 [16384, 1024], P('dp'), may hold values from -16 to 16
Outputs:
- output: bfloat16 [16384, 1024], P('dp')
- input_gradient: float32 [16384, 1024], P('dp')
- attention_gain_gradient: float32 [2, 1024], P(None, 'dp')
- query_gradient: float32 [2, 1024, 1024], P(None, 'dp', 'tensor')
- key_gradient: float32 [2, 1024, 512], P(None, 'dp', 'tensor')
- value_gradient: float32 [2, 1024, 512], P(None, 'dp', 'tensor')
- projection_gradient: float32 [2, 1024, 1024], P(None, 'tensor', 'dp')
- expert_gain_gradient: float32 [2, 1024], P(None, 'dp')
- router_gradient: float32 [2, 1024, 4], P(None, 'dp')
- gate_gradient: float32 [2, 4, 1024, 512], P(None, None, 'dp', 'tensor')
- up_gradient: float32 [2, 4, 1024, 512], P(None, None, 'dp', 'tensor')
- down_gradient: float32 [2, 4, 512, 1024], P(None, None, 'tensor', 'dp')
Inputs may be any that keep to these rules, and one draw needn't show every extreme that they name: `routes`: in each layer every token names 2 different experts. `segments`: numbers never fall along a sequence; a document has at most half of 256 tokens.
All inputs are finite; a program needn't handle non-finite values.
Results may differ from a plain program's by a relative error of at most 0.022.
The roundings to bfloat16 on the way count: a program that leaves them out, or rounds other values in their place, can miss the bound.
Values sent between devices are 32-bit elements; how exact they have to be, the bound alone decides.
No kernel may reach another device: no remote copies, remote signals or barrier semaphores. Data moves between devices by JAX's collectives and lax.ppermute only.
A program may use at most 256 MiB of HBM per device.

v0:
```python
import jax
import jax.numpy as jnp
from jax import lax
from jax.sharding import Mesh
from jax.sharding import PartitionSpec as P

HEAD_SIZE = 64
ROW_BLOCK = 128
DP = ("dp_0", "dp_1", "dp_2", "dp_3")


EPSILON = 1e-06
THETA = 10000.0
EXCLUDED = -1e30
HIGHEST = lax.Precision.HIGHEST


def copy_for_each(array, axis):
    copies = jnp.broadcast_to(array, (lax.axis_size(axis), *array.shape))
    return lax.all_to_all(copies, axis, split_axis=0, concat_axis=0, tiled=True)


def taken_together(array, axis):
    everything = copy_for_each(array, axis)
    return jnp.sum(everything, axis=0)


def cut_along(array, dim, size):
    dims = array.shape
    blocks = array.reshape(*dims[:dim], size, dims[dim] // size, *dims[dim + 1 :])
    return jnp.moveaxis(blocks, dim, 0)


def scatter_pairs(array, chips, core, dim):
    sizes = (lax.axis_size(chips), lax.axis_size(core))
    blocks = cut_along(array, dim, sizes[0] * sizes[1])
    inside = blocks.shape[1:]
    blocks = blocks.reshape(*sizes, *inside).swapaxes(0, 1).reshape(-1, *inside)
    blocks = lax.psum_scatter(blocks, core, scatter_dimension=0, tiled=True)
    return lax.psum_scatter(blocks, chips, scatter_dimension=0, tiled=True)[0]


def rope_tables(token_length, head_width):
    half_width = head_width // 2
    frequency = THETA ** (-2.0 * jnp.arange(half_width, dtype=jnp.float32) / head_width)
    angles = jnp.arange(token_length, dtype=jnp.float32)[:, None] * frequency[None, :]
    cosine_table = jnp.concatenate([jnp.cos(angles), jnp.cos(angles)], axis=1)[:, None, :]
    sine_table = jnp.concatenate([jnp.sin(angles), jnp.sin(angles)], axis=1)[:, None, :]
    return (cosine_table, sine_table)


def rotate(field, cosine_table, sine_table):
    half_width = field.shape[-1] // 2
    turned = jnp.concatenate([-field[..., half_width:], field[..., :half_width]], axis=-1)
    return field * cosine_table + turned * sine_table


def unrotate(gradient, cosine_table, sine_table):
    half_width = gradient.shape[-1] // 2
    scaled = gradient * sine_table
    turned = jnp.concatenate([scaled[..., half_width:], -scaled[..., :half_width]], axis=-1)
    return gradient * cosine_table + turned


def normalize(stream, gain):
    factor = lax.rsqrt(jnp.mean(stream * stream, axis=-1, keepdims=True) + EPSILON)
    return (stream * factor * gain, factor)


def normalize_back(stream, factor, gain, gradient):
    weighted = gradient * gain
    inner = jnp.sum(weighted * stream, axis=-1, keepdims=True) / stream.shape[-1]
    stream_change = factor * weighted - stream * (factor * factor * factor) * inner
    return (stream_change, jnp.sum(gradient * stream * factor, axis=0))


def pack_major(members, positions):
    flattened = [
        jnp.moveaxis(member, position, 0).reshape(member.shape[position], -1)
        for member, position in zip(members, positions)
    ]
    return jnp.concatenate(flattened, axis=1)


def unpack_major(summed, members, positions):
    pieces = []
    column_start = 0
    for member, position in zip(members, positions):
        rest_shape = tuple(
            (extent for index_number, extent in enumerate(member.shape) if index_number != position)
        )
        column_count = 1
        for extent in rest_shape:
            column_count = column_count * extent
        segment_piece = summed[:, column_start : column_start + column_count].reshape(
            (summed.shape[0],) + rest_shape
        )
        column_start = column_start + column_count
        pieces.append(jnp.moveaxis(segment_piece, 0, position))
    return tuple(pieces)


def block_logits(query_block, key_matrix_rows, segment, offset, score_scale):
    rows_per_block = query_block.shape[0]
    scores = (
        jnp.einsum(
            "qkgd,skd->kgqs", query_block, key_matrix_rows, preferred_element_type=jnp.float32
        )
        * score_scale
    )
    rows_at = offset + jnp.arange(rows_per_block, dtype=jnp.int32)
    columns_at = jnp.arange(key_matrix_rows.shape[0], dtype=jnp.int32)
    allowed = (columns_at[None, :] <= rows_at[:, None]) & (segment[:, None] == segment[None, :])
    return jnp.where(allowed, scores, EXCLUDED)


def attend_forward(query_rows, key_matrix_rows, value_matrix_rows, segment, score_scale):
    token_length = query_rows.shape[0]
    rows_per_block = min(512, token_length)
    starts = jnp.arange(token_length // rows_per_block, dtype=jnp.int32) * rows_per_block
    query_block_grid = query_rows.reshape(
        (token_length // rows_per_block, rows_per_block) + query_rows.shape[1:]
    )

    def one_block(inputs):
        query_block, offset = inputs
        masked = block_logits(query_block, key_matrix_rows, segment, offset, score_scale)
        largest = jnp.max(masked, axis=-1, keepdims=True)
        shifted = jnp.exp(masked - largest)
        totals = jnp.sum(shifted, axis=-1, keepdims=True)
        softmax_low = (shifted / totals).astype(jnp.bfloat16)
        mixture = jnp.einsum(
            "kgqs,skd->qkgd", softmax_low, value_matrix_rows, preferred_element_type=jnp.float32
        )
        return (mixture.astype(jnp.bfloat16), (largest + jnp.log(totals))[..., 0])

    mixture, log_totals = lax.map(one_block, (query_block_grid, starts))
    return (mixture.reshape(query_rows.shape), log_totals)


def attend_backward(
    query_rows, key_matrix_rows, value_matrix_rows, segment, log_totals, mixture_change, score_scale
):
    token_length = query_rows.shape[0]
    rows_per_block = min(512, token_length)
    starts = jnp.arange(token_length // rows_per_block, dtype=jnp.int32) * rows_per_block
    query_block_grid = query_rows.reshape(
        (token_length // rows_per_block, rows_per_block) + query_rows.shape[1:]
    )
    change_grid = mixture_change.reshape(
        (token_length // rows_per_block, rows_per_block) + query_rows.shape[1:]
    )

    def one_block(totals, inputs):
        key_total, value_total = totals
        query_block, change_block, log_block, offset = inputs
        masked = block_logits(query_block, key_matrix_rows, segment, offset, score_scale)
        probable = jnp.exp(masked - log_block[..., None])
        softmax_low = probable.astype(jnp.bfloat16)
        prob_change = jnp.einsum(
            "qkgd,skd->kgqs", change_block, value_matrix_rows, preferred_element_type=jnp.float32
        )
        inner = jnp.sum(probable * prob_change, axis=-1, keepdims=True)
        score_change = (probable * (prob_change - inner)).astype(jnp.bfloat16)
        query_change = (
            jnp.einsum(
                "kgqs,skd->qkgd", score_change, key_matrix_rows, preferred_element_type=jnp.float32
            )
            * score_scale
        )
        key_total = (
            key_total
            + jnp.einsum(
                "kgqs,qkgd->skd", score_change, query_block, preferred_element_type=jnp.float32
            )
            * score_scale
        )
        value_total = value_total + jnp.einsum(
            "kgqs,qkgd->skd", softmax_low, change_block, preferred_element_type=jnp.float32
        )
        return ((key_total, value_total), query_change)

    empty_rows = jnp.zeros(key_matrix_rows.shape, jnp.float32)
    (key_total, value_total), query_change = lax.scan(
        one_block, (empty_rows, empty_rows), (query_block_grid, change_grid, log_totals, starts)
    )
    return (query_change.reshape(query_rows.shape), key_total, value_total)


def arrange(route_rows, experts, row_block):
    token_count, per_token = route_rows.shape
    flat_routes = route_rows.reshape(-1)
    chosen = (flat_routes[:, None] == jnp.arange(experts, dtype=jnp.int32)[None, :]).astype(
        jnp.int32
    )
    counts = jnp.sum(chosen, axis=0)
    padded = (counts + row_block - 1) // row_block * row_block
    block_ends = jnp.cumsum(padded)
    starts = block_ends - padded
    earlier = jnp.cumsum(chosen, axis=0) - chosen
    places = jnp.sum(chosen * (earlier + starts[None, :]), axis=1)
    capacity = token_count * per_token + experts * row_block
    sources = (
        jnp.full((capacity,), token_count * per_token, jnp.int32)
        .at[places]
        .set(jnp.arange(token_count * per_token, dtype=jnp.int32))
    )
    block_first = jnp.arange(capacity // row_block, dtype=jnp.int32) * row_block
    block_owner = jnp.minimum(
        jnp.sum((block_first[:, None] >= block_ends[None, :]).astype(jnp.int32), axis=1),
        experts - 1,
    )
    return (places, sources, block_owner)


def add_at(totals, index_value, term):
    current = lax.dynamic_index_in_dim(totals, index_value, 0, keepdims=False)
    return lax.dynamic_update_index_in_dim(totals, current + term, index_value, 0)


def expert_forward(row_grid, block_owner, gate_weights, up_weights, down_weights):

    def one_block(inputs):
        rows_block, owner_id = inputs
        weight_gate = lax.dynamic_index_in_dim(gate_weights, owner_id, 0, keepdims=False)
        weight_up = lax.dynamic_index_in_dim(up_weights, owner_id, 0, keepdims=False)
        weight_down = lax.dynamic_index_in_dim(down_weights, owner_id, 0, keepdims=False)
        gate_in = jnp.dot(rows_block, weight_gate, preferred_element_type=jnp.float32)
        linear = jnp.dot(rows_block, weight_up, preferred_element_type=jnp.float32)
        activation = (jax.nn.silu(gate_in) * linear).astype(jnp.bfloat16)
        partial_out = jnp.dot(activation, weight_down, preferred_element_type=jnp.float32)
        return (gate_in, linear, activation, partial_out)

    return lax.map(one_block, (row_grid, block_owner))


def expert_backward(
    row_grid,
    block_owner,
    gate_in,
    linear,
    activation,
    change_grid,
    gate_weights,
    up_weights,
    down_weights,
):

    def one_block(totals, inputs):
        gate_total, up_total, down_total = totals
        rows_block, owner_id, gate_block, linear_block, active_block, incoming = inputs
        weight_gate = lax.dynamic_index_in_dim(gate_weights, owner_id, 0, keepdims=False)
        weight_up = lax.dynamic_index_in_dim(up_weights, owner_id, 0, keepdims=False)
        weight_down = lax.dynamic_index_in_dim(down_weights, owner_id, 0, keepdims=False)
        down_total = add_at(
            down_total,
            owner_id,
            jnp.einsum("rf,rd->fd", active_block, incoming, preferred_element_type=jnp.float32),
        )
        active_change = jnp.einsum(
            "rd,fd->rf", incoming, weight_down, preferred_element_type=jnp.float32
        )
        squashed = jax.nn.sigmoid(gate_block)
        gate_change = (
            active_change * linear_block * squashed * (1.0 + gate_block * (1.0 - squashed))
        ).astype(jnp.bfloat16)
        linear_change = (active_change * gate_block * squashed).astype(jnp.bfloat16)
        gate_total = add_at(
            gate_total,
            owner_id,
            jnp.einsum("rd,rf->df", rows_block, gate_change, preferred_element_type=jnp.float32),
        )
        up_total = add_at(
            up_total,
            owner_id,
            jnp.einsum("rd,rf->df", rows_block, linear_change, preferred_element_type=jnp.float32),
        )
        row_change = jnp.einsum(
            "rf,df->rd", gate_change, weight_gate, preferred_element_type=jnp.float32
        )
        row_change = row_change + jnp.einsum(
            "rf,df->rd", linear_change, weight_up, preferred_element_type=jnp.float32
        )
        return ((gate_total, up_total, down_total), row_change)

    empty_in = jnp.zeros(gate_weights.shape, jnp.float32)
    empty_out = jnp.zeros(down_weights.shape, jnp.float32)
    return lax.scan(
        one_block,
        (empty_in, empty_in, empty_out),
        (row_grid, block_owner, gate_in, linear, activation, change_grid),
    )


def shards(
    tokens,
    segments,
    routes,
    norm_attention,
    query_weight,
    key_matrix,
    value_matrix,
    output_weight,
    norm_experts,
    router_weight,
    gate_weight,
    up_weight,
    down_weight,
    cotangent,
):
    token_length, features = tokens.shape
    layers = query_weight.shape[0]
    head_count = query_weight.shape[2] // HEAD_SIZE
    key_heads = key_matrix.shape[2] // HEAD_SIZE
    group_width = head_count // key_heads
    experts = gate_weight.shape[1]
    per_token = routes.shape[2]
    score_scale = HEAD_SIZE ** (-0.5)
    segment = segments[0]
    cosine_table, sine_table = rope_tables(token_length, HEAD_SIZE)
    block_count = (token_length * per_token + experts * ROW_BLOCK) // ROW_BLOCK
    stream = tokens.astype(jnp.float32)
    stored = []
    for layer_index in range(layers):
        gain_attention = norm_attention[layer_index].astype(jnp.float32)
        normed, attention_factor = normalize(stream, gain_attention)
        attention_inputs = normed.astype(jnp.bfloat16)
        query_rows = jnp.dot(
            attention_inputs, query_weight[layer_index], preferred_element_type=jnp.float32
        ).reshape(token_length, head_count, HEAD_SIZE)
        key_matrix_rows = jnp.dot(
            attention_inputs, key_matrix[layer_index], preferred_element_type=jnp.float32
        ).reshape(token_length, key_heads, HEAD_SIZE)
        value_matrix_rows = (
            jnp.dot(attention_inputs, value_matrix[layer_index], preferred_element_type=jnp.float32)
            .astype(jnp.bfloat16)
            .reshape(token_length, key_heads, HEAD_SIZE)
        )
        query_rows = (
            rotate(query_rows, cosine_table, sine_table)
            .astype(jnp.bfloat16)
            .reshape(token_length, key_heads, group_width, HEAD_SIZE)
        )
        key_matrix_rows = rotate(key_matrix_rows, cosine_table, sine_table).astype(jnp.bfloat16)
        mixture, log_totals = attend_forward(
            query_rows, key_matrix_rows, value_matrix_rows, segment, score_scale
        )
        mixture = mixture.reshape(token_length, head_count * HEAD_SIZE)
        branch = jnp.dot(mixture, output_weight[layer_index], preferred_element_type=jnp.float32)
        middle = stream + taken_together(branch, "tensor")
        gain_experts = norm_experts[layer_index].astype(jnp.float32)
        normed, expert_factor = normalize(middle, gain_experts)
        expert_input = normed.astype(jnp.bfloat16)
        route_rows = routes[layer_index]
        chosen = (
            route_rows[:, :, None] == jnp.arange(experts, dtype=jnp.int32)[None, None, :]
        ).astype(jnp.float32)
        logits = jnp.dot(
            expert_input, router_weight[layer_index], preferred_element_type=jnp.float32
        )
        gates = jax.nn.softmax(jnp.sum(chosen * logits[:, None, :], axis=-1), axis=-1)
        places, sources, block_owner = arrange(route_rows, experts, ROW_BLOCK)
        padded_input = jnp.concatenate(
            [expert_input, jnp.zeros((1, features), jnp.bfloat16)], axis=0
        )
        row_grid = padded_input[sources // per_token].reshape(block_count, ROW_BLOCK, features)
        gate_in, linear, activation, partial_out = expert_forward(
            row_grid,
            block_owner,
            gate_weight[layer_index],
            up_weight[layer_index],
            down_weight[layer_index],
        )
        picked = partial_out.reshape(-1, features)[places].reshape(
            token_length, per_token, features
        )
        combined = jnp.sum(gates[:, :, None] * picked, axis=1)
        stored.append(
            (
                stream,
                attention_factor,
                attention_inputs,
                query_rows,
                key_matrix_rows,
                value_matrix_rows,
                log_totals,
                mixture,
                middle,
                expert_factor,
                expert_input,
                chosen,
                gates,
                places,
                sources,
                block_owner,
                row_grid,
                gate_in,
                linear,
                activation,
                picked,
            )
        )
        stream = middle + taken_together(combined, "tensor")
    output = stream.astype(jnp.bfloat16)
    gradient = cotangent.astype(jnp.float32)
    results = [None] * layers
    for layer_index in reversed(range(layers)):
        (
            stream,
            attention_factor,
            attention_inputs,
            query_rows,
            key_matrix_rows,
            value_matrix_rows,
            log_totals,
            mixture,
            middle,
            expert_factor,
            expert_input,
            chosen,
            gates,
            places,
            sources,
            block_owner,
            row_grid,
            gate_in,
            linear,
            activation,
            picked,
        ) = stored[layer_index]
        gain_attention = norm_attention[layer_index].astype(jnp.float32)
        gain_experts = norm_experts[layer_index].astype(jnp.float32)
        route_change = (
            (gates[:, :, None] * gradient[:, None, :])
            .astype(jnp.bfloat16)
            .reshape(token_length * per_token, features)
        )
        route_change = jnp.concatenate(
            [route_change, jnp.zeros((1, features), jnp.bfloat16)], axis=0
        )
        change_grid = route_change[sources].reshape(block_count, ROW_BLOCK, features)
        gate_part = jnp.sum(gradient[:, None, :] * picked, axis=-1)
        (gate_total, up_total, down_total), row_change = expert_backward(
            row_grid,
            block_owner,
            gate_in,
            linear,
            activation,
            change_grid,
            gate_weight[layer_index],
            up_weight[layer_index],
            down_weight[layer_index],
        )
        input_part = jnp.sum(
            row_change.reshape(-1, features)[places].reshape(token_length, per_token, features),
            axis=1,
        )
        input_change, gate_change = lax.psum((input_part, gate_part), "tensor")
        pick_change = gates * (gate_change - jnp.sum(gates * gate_change, axis=-1, keepdims=True))
        logit_change = jnp.sum(chosen * pick_change[:, :, None], axis=1)
        router_full = router_weight[layer_index].astype(jnp.float32)
        input_change = input_change + jnp.einsum(
            "te,de->td", logit_change, router_full, precision=HIGHEST
        )
        router_total = jnp.einsum(
            "td,te->de", expert_input.astype(jnp.float32), logit_change, precision=HIGHEST
        )
        middle_change, expert_gain_total = normalize_back(
            middle, expert_factor, gain_experts, input_change
        )
        gradient = gradient + middle_change
        output_change = gradient.astype(jnp.bfloat16)
        projection_total = jnp.einsum(
            "tq,td->qd", mixture, output_change, preferred_element_type=jnp.float32
        )
        mixture_change = jnp.einsum(
            "td,qd->tq",
            output_change,
            output_weight[layer_index],
            preferred_element_type=jnp.float32,
        ).astype(jnp.bfloat16)
        mixture_change = mixture_change.reshape(token_length, key_heads, group_width, HEAD_SIZE)
        query_change, key_change, value_change = attend_backward(
            query_rows,
            key_matrix_rows,
            value_matrix_rows,
            segment,
            log_totals,
            mixture_change,
            score_scale,
        )
        query_change = (
            unrotate(
                query_change.reshape(token_length, head_count, HEAD_SIZE), cosine_table, sine_table
            )
            .astype(jnp.bfloat16)
            .reshape(token_length, head_count * HEAD_SIZE)
        )
        key_change = (
            unrotate(key_change, cosine_table, sine_table)
            .astype(jnp.bfloat16)
            .reshape(token_length, key_heads * HEAD_SIZE)
        )
        value_change = value_change.astype(jnp.bfloat16).reshape(
            token_length, key_heads * HEAD_SIZE
        )
        query_total = jnp.einsum(
            "td,tq->dq", attention_inputs, query_change, preferred_element_type=jnp.float32
        )
        key_total = jnp.einsum(
            "td,tq->dq", attention_inputs, key_change, preferred_element_type=jnp.float32
        )
        value_total = jnp.einsum(
            "td,tq->dq", attention_inputs, value_change, preferred_element_type=jnp.float32
        )
        attention_part = jnp.einsum(
            "tq,dq->td", query_change, query_weight[layer_index], preferred_element_type=jnp.float32
        )
        attention_part = attention_part + jnp.einsum(
            "tq,dq->td", key_change, key_matrix[layer_index], preferred_element_type=jnp.float32
        )
        attention_part = attention_part + jnp.einsum(
            "tq,dq->td", value_change, value_matrix[layer_index], preferred_element_type=jnp.float32
        )
        attention_change = taken_together(attention_part, "tensor")
        stream_change, attention_gain_total = normalize_back(
            stream, attention_factor, gain_attention, attention_change
        )
        gradient = gradient + stream_change
        layer_totals = (
            attention_gain_total,
            query_total,
            key_total,
            value_total,
            projection_total,
            expert_gain_total,
            router_total,
            gate_total,
            up_total,
            down_total,
        )
        results[layer_index] = layer_totals
    stacked = [
        jnp.stack([results[layer_index][member] for layer_index in range(layers)])
        for member in range(10)
    ]
    stacked_positions = (1, 1, 1, 1, 2, 1, 1, 2, 2, 3)
    summed_all = scatter_pairs(
        pack_major(stacked, stacked_positions), ("dp_0", "dp_1", "dp_2"), "dp_3", 0
    )
    stacked = list(unpack_major(summed_all, stacked, stacked_positions))
    return (
        output,
        gradient,
        stacked[0],
        stacked[1],
        stacked[2],
        stacked[3],
        stacked[4],
        stacked[5],
        stacked[6],
        stacked[7],
        stacked[8],
        stacked[9],
    )


def solution(mesh):
    torus = Mesh(
        mesh.devices.reshape(4, 2, 4, 2, mesh.shape["tensor"]),
        ("dp_0", "dp_1", "dp_2", "dp_3", "tensor"),
    )
    in_specs = (
        P(DP, None),
        P(DP, None),
        P(None, DP, None),
        P(),
        P(None, None, "tensor"),
        P(None, None, "tensor"),
        P(None, None, "tensor"),
        P(None, "tensor", None),
        P(),
        P(),
        P(None, None, None, "tensor"),
        P(None, None, None, "tensor"),
        P(None, None, "tensor", None),
        P(DP, None),
    )
    out_specs = (
        P(DP, None),
        P(DP, None),
        P(None, DP),
        P(None, DP, "tensor"),
        P(None, DP, "tensor"),
        P(None, DP, "tensor"),
        P(None, "tensor", DP),
        P(None, DP),
        P(None, DP, None),
        P(None, None, DP, "tensor"),
        P(None, None, DP, "tensor"),
        P(None, None, "tensor", DP),
    )
    return jax.shard_map(
        shards, mesh=torus, in_specs=in_specs, out_specs=out_specs, check_vma=False
    )
```

profile of v0, /device:TPU:0, one launch (start us, length us, event | category | flops | bytes accessed | tf_op | source)
XLA Modules:
  0.0 1324.6 jit_solution(1282946692361121492)
XLA Ops:
  23.4 3.9 all-to-all-start
  30.0 2.7 scatter_custom_fusion
  34.0 5.0 slice_bitcast_fusion
  40.3 3.4 slice_bitcast_fusion.1
  43.7 8.7 all-to-all-done
  55.8 5.3 gather_fusion
  63.4 2.5 broadcast.591.clone
  65.9 69.5 %while.14 = (s32[]{:T(128)}, f32[8,128,256]{2,1,0:T(8,128)}, f32[8,128,256]{2,1,0:T(8,128)}, bf16[8,128,256]{2,1,0:T(8,128)(2,1)S(1)}, f32[8,128,1024]{2,1,0:T(8...) while((s32[]{:T(128)}, f32[8,128,256]{2,1,0:T(8,128)}, ...), condition=%wide.region_16.17_spmd, body=%wide.region_15.16_spmd.sunk | while | flops 201523200 | bytes 3607743 | solution.py:234
  135.4 6.0 gather_fusion.1
  141.4 3.5 reshape.681
  145.4 4.3 multiply_reduce_fusion.3
  151.3 5.1 all-to-all-start.1
  163.7 3.7 mul.815
  167.3 13.2 all-to-all-done.1
  180.6 2.8 reduce_sum.397
  192.7 4.8 all-to-all-start.2
  200.3 20.6 %all-to-all-done.2 = f32[2,256,1024]{2,1,0:T(8,128)} async-done(((f32[2,256,1024]{2,1,0:T(8,128)}), f32[2,256,1024]{2,1,0:T(8,128)}, u32[]{:S(2)}, u32[]{:S(2)}) %all-to-all-start.2) | async-done | bytes 2097184 | tf_op jit(solution)/shard_map/all_to_all | solution.py:20
  220.9 2.9 reduce_sum.400
  227.3 5.8 gather_fusion.2
  237.9 69.5 %while.15 = (s32[]{:T(128)}, f32[8,128,256]{2,1,0:T(8,128)}, f32[8,128,256]{2,1,0:T(8,128)}, bf16[8,128,256]{2,1,0:T(8,128)(2,1)S(1)}, f32[8,128,1024]{2,1,0:T(8...) while((s32[]{:T(128)}, f32[8,128,256]{2,1,0:T(8,128)}, ...), condition=%wide.region_35.36_spmd, body=%wide.region_34.35_spmd.sunk | while | flops 201523200 | bytes 3607743 | solution.py:234
  310.0 5.3 gather_fusion.4
  320.0 2.6 broadcast.610.clone
  325.0 139.6 %while.16 = (s32[]{:T(128)}, f32[4,1024,256]{2,1,0:T(8,128)}, f32[4,1024,256]{2,1,0:T(8,128)}, f32[4,256,1024]{2,1,0:T(8,128)}, f32[8,128,1024]{2,1,0:T(8,128)},...) while((s32[]{:T(128)}, f32[4,1024,256]{2,1,0:T(8,128)}, ...), condition=%wide.region_39.40_spmd, body=%wide.region_38.39_spmd.sunk | while | flops 403996672 | bytes 17501432 | solution.py:288
  464.7 5.8 gather_fusion.5
  470.5 3.5 reshape.690
  474.0 5.1 reduce_sum.410
  479.1 5.8 gather_fusion.3
  484.9 3.5 reshape.687
  488.4 5.2 multiply_reduce_fusion.1
  495.4 4.9 all-to-all-start.3
  500.4 35.0 %psum.29 = f32[256,2]{0,1:T(2,128)S(1)} all-reduce(f32[256,2]{0,1:T(2,128)S(1)} %copy.194), channel_id=1, replica_groups=mesh['dp_0'=4,'dp_1'=2,'dp_2'=4,'dp_3'=2,'tensor'=2] {'tensor'}, use_global_device_ids=true, to_apply=%region_43.44 | all-reduce | flops 512 | bytes 4096 | tf_op jit(solution)/shard_map/psum | solution.py:458
  537.6 3.7 multiply_reduce_fusion.4
  541.2 2.8 reduce_sum.409
  544.1 3.3 subtract_add_fusion.2
  558.9 4.9 all-to-all-start.4
  568.9 20.3 %all-to-all-done.4 = f32[2,256,1024]{2,1,0:T(8,128)} async-done(((f32[2,256,1024]{2,1,0:T(8,128)}), f32[2,256,1024]{2,1,0:T(8,128)}, u32[]{:S(2)}, u32[]{:S(2)}) %all-to-all-start.4) | async-done | bytes 2097184 | tf_op jit(solution)/shard_map/all_to_all | solution.py:20
  597.9 3.9 mul.855
  603.6 5.3 gather_fusion.6
  618.6 139.3 %while.17 = (s32[]{:T(128)}, f32[4,1024,256]{2,1,0:T(8,128)}, f32[4,1024,256]{2,1,0:T(8,128)}, f32[4,256,1024]{2,1,0:T(8,128)}, f32[8,128,1024]{2,1,0:T(8,128)},...) while((s32[]{:T(128)}, f32[4,1024,256]{2,1,0:T(8,128)}, ...), condition=%wide.region_51.52_spmd, body=%wide.region_50.51_spmd.sunk | while | flops 403996672 | bytes 17501432 | solution.py:288
  757.9 5.0 gather_fusion.7
  765.2 5.1 reduce_sum.418
  770.4 5.3 psum.31
  777.6 7.6 maximum_bitcast_fusion
  785.3 12.1 copy.209
  797.3 11.0 concatenate.93
  808.3 7.3 maximum_bitcast_fusion.1
  815.6 12.0 copy.210
  827.6 10.7 concatenate.94
  838.4 8.4 maximum_bitcast_fusion.2
  846.8 10.2 copy.211
  857.0 11.0 concatenate.95
  868.1 2.8 multiply_reduce_fusion.5
  884.1 5.0 all-to-all-start.5
  891.8 5.2 copy.205
  897.1 6.9 concatenate.87
  905.8 2.7 concatenate.88
  909.8 3.0 copy.207
  912.8 4.0 concatenate.89
  920.8 7.2 copy.208
  928.0 6.6 concatenate.90
  939.1 49.3 %concatenate.96 = f32[32,2,16,9228]{3,2,1,0:T(8,128)} concatenate(f32[32,2,16,2]{3,2,1,0:T(8,128)} %bitcast.817, f32[32,2,16,1024]{3,2,1,0:T(8,128)} %concatenate.87, f32[32,2,16,512]{3,2,1,0:T(8,128)} %concatenate.88, f32[32,2,16,512]{3,2,1,0:T(8,128)} %concatenate.89, f32[32,2,16,1024]{3,2,1,0:T(8,128)} %concatenate.90, f32[32,2,16,2]{3,2,1,0:T(8,128)} %bitcast.816, ...), dimensions={3} | concatenate | bytes 75595776 | tf_op jit(solution)/shard_map/concatenate | solution.py:82
  988.3 26.3 %copy.215 = f32[2,32,16,9228]{3,2,1,0:T(8,128)} copy(f32[2,32,16,9228]{3,2,0,1:T(8,128)} %bitcast.791) | data formatting | bytes 75595776 | tf_op jit(solution)/shard_map/transpose | solution.py:38
  1014.7 54.1 %reduce-scatter.3.cloned.1.call-done = f32[32,16,9228]{2,1,0:T(8,128)} async-done(((f32[64,16,9228]{2,1,0:T(8,128)}), f32[32,16,9228]{2,1,0:T(8,128)}) %reduce-scatter.3.cloned.1.call-update) | async-done | bytes 18898960 | tf_op jit(solution)/shard_map/reduce_scatter | solution.py:39
  1070.7 235.4 %reduce-scatter.5.cloned.1.call-done = f32[1,16,9228]{2,1,0:T(8,128)} async-done(((f32[32,16,9228]{2,1,0:T(8,128)}), f32[1,16,9228]{2,1,0:T(8,128)}) %reduce-scatter.5.cloned.1.call-update) | async-done | bytes 590608 | tf_op jit(solution)/shard_map/reduce_scatter | solution.py:40
  (730 shorter events, 506.7 us)
Async XLA Ops:
  8.0 7.5 copy-start.74
  8.0 177.5 %copy-start.91 = (f32[1,1024]{1,0:T(1,128)}, f32[1,1024]{1,0:T(1,128)S(1)}, u32[]{:S(2)}) copy-start(f32[1,1024]{1,0:T(1,128)S(1)} %get-tuple-element.617) | copy-start | bytes 12292
  9.9 5.7 copy-start.95
  23.4 28.9 %all-to-all-start = ((f32[2,256,1024]{2,1,0:T(8,128)}), f32[2,256,1024]{2,1,0:T(8,128)S(1)}, u32[]{:S(2)}, u32[]{:S(2)}) async-start(f32[2,256,1024]{2,1,0:T(8,128)} %broadcast_in_dim.208), calls=%async_computation | async-start | bytes 4194304 | tf_op jit(solution)/shard_map/all_to_all | solution.py:20
  27.4 117.7 %copy-start.107 = (s32[256,2]{0,1:T(2,128)}, s32[256,2]{0,1:T(2,128)S(1)}, u32[]{:S(2)}) copy-start(s32[256,2]{0,1:T(2,128)S(1)} %get-tuple-element.612) | copy-start | bytes 6148
  27.4 199.0 %copy-start.109 = (s32[256,2]{0,1:T(2,128)}, s32[256,2]{0,1:T(2,128)S(1)}, u32[]{:S(2)}) copy-start(s32[256,2]{0,1:T(2,128)S(1)} %get-tuple-element.611) | copy-start | bytes 6148
  27.9 27.8 %copy-start.89 = (f32[1,1024]{1,0:T(1,128)}, f32[1,1024]{1,0:T(1,128)S(1)}, u32[]{:S(2)}) copy-start(f32[1,1024]{1,0:T(1,128)S(1)} %get-tuple-element.616) | copy-start | bytes 12292
  27.9 197.9 %copy-start.93 = (f32[1,1024]{1,0:T(1,128)}, f32[1,1024]{1,0:T(1,128)S(1)}, u32[]{:S(2)}) copy-start(f32[1,1024]{1,0:T(1,128)S(1)} %get-tuple-element.615) | copy-start | bytes 12292
  34.0 101.4 %copy-start.114 = (s32[1024]{0:T(1024)}, s32[1024]{0:T(1024)S(1)}, u32[]{:S(2)}) copy-start(s32[1024]{0:T(1024)S(1)} %pad_clamp_fusion.1) | copy-start | bytes 12292
  34.0 6.2 copy-start.42
  55.0 128.4 %copy-start.2 = (f32[256,1024]{1,0:T(8,128)}, f32[256,1024]{1,0:T(8,128)S(1)}, u32[]{:S(2)}) copy-start(f32[256,1024]{1,0:T(8,128)S(1)} %get-tuple-element.543) | copy-start | bytes 3145732
  55.6 5.6 copy-start.124
  55.8 89.1 %copy-start.28 = (bf16[256,1024]{1,0:T(8,128)(2,1)}, bf16[256,1024]{1,0:T(8,128)(2,1)S(1)}, u32[]{:S(2)}) copy-start(bf16[256,1024]{1,0:T(8,128)(2,1)S(1)} %multiply_convert_fusion.6) | copy-start | bytes 1572868
  135.4 6.0 copy-start.50
  135.4 6.0 copy-start.134
  145.1 6.1 copy-start.82
  145.2 6.1 copy-start.103
  145.2 6.1 copy-start.120
  145.4 5.9 copy-start.52
  151.3 29.3 %all-to-all-start.1 = ((f32[2,256,1024]{2,1,0:T(8,128)}), f32[2,256,1024]{2,1,0:T(8,128)}, u32[]{:S(2)}, u32[]{:S(2)}) async-start(f32[2,256,1024]{2,1,0:T(8,128)} %broadcast_in_dim.210), calls=%async_computation.1 | async-start | bytes 4194304 | tf_op jit(solution)/shard_map/all_to_all | solution.py:20
  192.7 28.1 %all-to-all-start.2 = ((f32[2,256,1024]{2,1,0:T(8,128)}), f32[2,256,1024]{2,1,0:T(8,128)}, u32[]{:S(2)}, u32[]{:S(2)}) async-start(f32[2,256,1024]{2,1,0:T(8,128)} %broadcast_in_dim.211), calls=%async_computation.2 | async-start | bytes 4194304 | tf_op jit(solution)/shard_map/all_to_all | solution.py:20
  197.6 26.2 %copy-start.5 = (f32[256,1024]{1,0:T(8,128)S(1)}, f32[256,1024]{1,0:T(8,128)}, u32[]{:S(2)}) copy-start(f32[256,1024]{1,0:T(8,128)} %copy-done.4) | copy-start | bytes 3145732
  197.6 340.0 %all-reduce.7.cloned.1.call-start = ((), (), s32[]{:S(2)}) async-start(), calls=%async_computation.8 | async-start | bytes 2097152 | tf_op jit(solution)/shard_map/psum | solution.py:458
  226.1 7.1 copy-start.30
  227.0 6.1 copy-start.122
  495.3 40.2 %copy-start.85 = (f32[256,2]{0,1:T(2,128)S(1)}, f32[256,2]{0,1:T(2,128)}, u32[]{:S(2)}) copy-start(f32[256,2]{0,1:T(2,128)} %copy-done.84) | copy-start | bytes 6148
  495.3 40.2 %copy-start.106 = (f32[256]{0:T(256)S(1)}, f32[256]{0:T(256)}, u32[]{:S(2)}) copy-start(f32[256]{0:T(256)} %copy-done.105) | copy-start | bytes 3076
  495.3 40.2 %copy-start.123 = (f32[256]{0:T(256)S(1)}, f32[256]{0:T(256)}, u32[]{:S(2)}) copy-start(f32[256]{0:T(256)} %copy-done.122) | copy-start | bytes 3076
  495.3 40.2 %copy-start.110 = (s32[256,2]{0,1:T(2,128)S(1)}, s32[256,2]{0,1:T(2,128)}, u32[]{:S(2)}) copy-start(s32[256,2]{0,1:T(2,128)} %copy-done.109) | copy-start | bytes 6148
  495.3 42.2 %copy-start.19 = (f32[256,1024]{1,0:T(8,128)S(1)}, f32[256,1024]{1,0:T(8,128)}, u32[]{:S(2)}) copy-start(f32[256,1024]{1,0:T(8,128)} %copy-done.18) | copy-start | bytes 3145732
  495.3 42.2 %copy-start.87 = (bf16[2,1024,4]{1,2,0:T(4,128)(2,1)S(1)}, bf16[2,1024,4]{1,2,0:T(4,128)(2,1)}, u32[]{:S(2)}) copy-start(bf16[2,1024,4]{1,2,0:T(4,128)(2,1)} %param.31) | copy-start | bytes 49156
  495.3 42.2 %copy-start.94 = (f32[1,1024]{1,0:T(1,128)S(1)}, f32[1,1024]{1,0:T(1,128)}, u32[]{:S(2)}) copy-start(f32[1,1024]{1,0:T(1,128)} %copy-done.93) | copy-start | bytes 12292
  495.4 42.2 %copy-start.127 = (f32[256]{0:T(256)S(1)}, f32[256]{0:T(256)}, u32[]{:S(2)}) copy-start(f32[256]{0:T(256)} %copy-done.126) | copy-start | bytes 3076
  495.4 45.9 %all-to-all-start.3 = ((f32[2,256,1024]{2,1,0:T(8,128)}), f32[2,256,1024]{2,1,0:T(8,128)}, u32[]{:S(2)}, u32[]{:S(2)}) async-start(f32[2,256,1024]{2,1,0:T(8,128)} %broadcast_in_dim.213), calls=%async_computation.3 | async-start | bytes 4194304 | tf_op jit(solution)/shard_map/all_to_all | solution.py:20
  535.5 8.5 copy-start.97
  547.4 19.7 %copy-start.16 = (f32[256,1024]{1,0:T(8,128)}, f32[256,1024]{1,0:T(8,128)S(1)}, u32[]{:S(2)}) copy-start(f32[256,1024]{1,0:T(8,128)S(1)} %get-tuple-element.568) | copy-start | bytes 3145732
  551.6 5.1 copy-start.60
  558.9 5.1 copy-start.100
  558.9 5.1 copy-start.53
  558.9 5.2 copy-start.31
  558.9 5.2 copy-start.98
  558.9 5.6 copy-start.11
  558.9 30.4 %all-to-all-start.4 = ((f32[2,256,1024]{2,1,0:T(8,128)}), f32[2,256,1024]{2,1,0:T(8,128)}, u32[]{:S(2)}, u32[]{:S(2)}) async-start(f32[2,256,1024]{2,1,0:T(8,128)} %broadcast_in_dim.215), calls=%async_computation.4 | async-start | bytes 4194304 | tf_op jit(solution)/shard_map/all_to_all | solution.py:20
  563.9 304.2 %all-reduce.9.cloned.1.call-start = ((), (), s32[]{:S(2)}) async-start(), calls=%async_computation.9 | async-start | bytes 2097152 | tf_op jit(solution)/shard_map/psum | solution.py:458
  568.9 22.2 %copy-start.6 = (f32[256,1024]{1,0:T(8,128)S(1)}, f32[256,1024]{1,0:T(8,128)}, u32[]{:S(2)}) copy-start(f32[256,1024]{1,0:T(8,128)} %copy-done.4) | copy-start | bytes 3145732
  568.9 22.2 %copy-start.92 = (f32[1,1024]{1,0:T(1,128)S(1)}, f32[1,1024]{1,0:T(1,128)}, u32[]{:S(2)}) copy-start(f32[1,1024]{1,0:T(1,128)} %copy-done.91) | copy-start | bytes 12292
  568.9 22.2 %copy-start.112 = (f32[256]{0:T(256)S(1)}, f32[256]{0:T(256)}, u32[]{:S(2)}) copy-start(f32[256]{0:T(256)} %copy-done.111) | copy-start | bytes 3076
  568.9 23.2 %copy-start.130 = (f32[256]{0:T(256)S(1)}, f32[256]{0:T(256)}, u32[]{:S(2)}) copy-start(f32[256]{0:T(256)} %get-tuple-element.623) | copy-start | bytes 3076
  618.6 139.3 %copy-start.115 = (s32[1024]{0:T(1024)S(1)}, s32[1024]{0:T(1024)}, u32[]{:S(2)}) copy-start(s32[1024]{0:T(1024)} %copy-done.114) | copy-start | bytes 12292
  765.2 10.6 copy-start.83
  765.2 10.6 copy-start.104
  765.2 10.6 copy-start.121
  765.2 10.6 copy-start.108
  765.2 10.6 copy-start.29
  857.0 11.1 copy-start.3
  857.0 11.1 copy-start.88
  857.0 11.1 copy-start.90
  857.0 11.1 copy-start.125
  884.1 51.6 %all-to-all-start.5 = ((f32[2,256,1024]{2,1,0:T(8,128)}), f32[2,256,1024]{2,1,0:T(8,128)}, u32[]{:S(2)}, u32[]{:S(2)}) async-start(f32[2,256,1024]{2,1,0:T(8,128)} %broadcast_in_dim.217), calls=%async_computation.5 | async-start | bytes 4194304 | tf_op jit(solution)/shard_map/all_to_all | solution.py:20
  889.1 179.7 %reduce-scatter.3.cloned.1.call-start = ((), (), s32[]{:S(2)}) async-start(), calls=%async_computation.10 | async-start | bytes 57409536 | tf_op jit(solution)/shard_map/reduce_scatter | solution.py:39
  897.1 6.9 copy-start.40
  928.0 6.6 copy-start.116
  928.0 6.6 copy-start.118
  1014.7 291.5 %reduce-scatter.5.cloned.1.call-start = ((), (), s32[]{:S(2)}) async-start(), calls=%async_computation.11 | async-start | bytes 19734528 | tf_op jit(solution)/shard_map/reduce_scatter | solution.py:40
  (82 other events, 173.5 us)
Sparse Core Ops, SparseCore 0:
  479.2 58.3 all-reduce.6
  770.5 47.6 all-reduce.8
  1014.8 53.9 reduce-scatter.2
  1071.2 234.8 reduce-scatter.4
where the time goes:
time: 1340 us; the launch traced here: 1320 us
  local copies, waits for them, and re-layouts  410 us (31%)
  waiting for transfers between devices  354 us (26%)
  matrix products  320 us (24%)
  other arithmetic  92.5 us (7%)
  loops' own time  62.4 us (5%)
  blocking collectives  40.4 us (3%)
  starting transfers between devices  28.8 us (2%)
  between operations  16.2 us (1%)
    reduce_scatter x1, waiting for transfers between devices, scatter_pairs(): return lax.psum_scatter(blocks, chips, scatter_dimension=0, tiled=True)[0]  235 us
    concatenate x12, local copies, waits for them, and re-layouts, pack_major(): return jnp.concatenate(flattened, axis=1)  106 us
    all_to_all x6, waiting for transfers between devices, copy_for_each(): return lax.all_to_all(copies, axis, split_axis=0, concat_axis=0, tiled=True)  62.8 us
    reduce_scatter x1, waiting for transfers between devices, scatter_pairs(): blocks = lax.psum_scatter(blocks, core, scatter_dimension=0, tiled=True)  54.1 us
    transpose x7, local copies, waits for them, and re-layouts, pack_major(): jnp.moveaxis(member, position, 0).reshape(member.shape[position], -1)  51.4 us
    dynamic_slice x32, local copies, waits for them, and re-layouts, add_at(): current = lax.dynamic_index_in_dim(totals, index_value, 0, keepdims=False)  48.1 us
    psum x2, blocking collectives, shards(): input_change, gate_change = lax.psum((input_part, gate_part), 'tensor')  40.4 us
    dot_general x16, matrix products, one_block(): jnp.einsum('rf,rd->fd', active_block, incoming, preferred_element_type=jn...  37.3 us
  transfers between devices with their start and end apart: 10, of which 7 were waited for; matrix products, arithmetic and copies ran while one was open for 14% of the time, Pallas kernels for 0%

commit v1 on v0

v1 whole, which is shorter than its diff:
```python
import functools

import jax
import jax.numpy as jnp
import numpy as np
from jax import lax
from jax.experimental import pallas as pl
from jax.experimental.pallas import tpu as pltpu
from jax.sharding import Mesh
from jax.sharding import PartitionSpec as P

HEAD_SIZE = 64
LANES = 128
STREAMS = 4
SMALL = 128
DP = ("dp_0", "dp_1", "dp_2", "dp_3")
DP_SIZES = (4, 2, 4, 2)
EPSILON = 1e-06
THETA = 10000.0
EXCLUDED = -1e30
F32 = jnp.float32
BF16 = jnp.bfloat16
MIB = 1024 * 1024

ORDERS = (
    (("x", "u"), ("z", "u"), ("x", "v"), ("z", "v")),
    (("z", "u"), ("x", "v"), ("z", "v"), ("x", "u")),
    (("x", "v"), ("z", "v"), ("x", "u"), ("z", "u")),
    (("z", "v"), ("x", "u"), ("z", "u"), ("x", "v")),
)


def pair_bit(index, kind):
    high = index // 2
    if kind == "v":
        return high
    return high ^ (index % 2)


def place(stream, x, yh, z):
    at = 0
    for ring, kind in ORDERS[stream]:
        at = at * 2 + pair_bit(x if ring == "x" else z, kind)
    return at * 2 + yh


def mm(a, b):
    return lax.dot_general(a, b, (((1,), (0,)), ((), ())), preferred_element_type=F32)


def mm_nt(a, b):
    return lax.dot_general(a, b, (((1,), (1,)), ((), ())), preferred_element_type=F32)


def mm_tn(a, b):
    return lax.dot_general(a, b, (((0,), (0,)), ((), ())), preferred_element_type=F32)


def row_factor(stream):
    return lax.rsqrt(jnp.mean(stream * stream, axis=-1, keepdims=True) + EPSILON)


def norm_back(stream, factor, gain, gradient):
    weighted = gradient * gain
    inner = jnp.sum(weighted * stream, axis=-1, keepdims=True) * (1.0 / stream.shape[-1])
    change = factor * weighted - stream * (factor * factor * factor) * inner
    return change, jnp.sum(gradient * stream * factor, axis=0, keepdims=True)


def lane_of(rows):
    return lax.broadcasted_iota(jnp.int32, (rows, LANES), 1)


def partner(block, lane):
    back = pltpu.roll(block, LANES - HEAD_SIZE // 2, 1)
    ahead = pltpu.roll(block, HEAD_SIZE // 2, 1)
    return jnp.where(lane % HEAD_SIZE < HEAD_SIZE // 2, back, ahead)


def both_heads(block, lane):
    rolled = pltpu.roll(block, HEAD_SIZE, 1)
    low = lane < HEAD_SIZE
    return jnp.where(low, block, rolled), jnp.where(low, rolled, block)


def stacked_pair(block, lane):
    zero = jnp.zeros_like(block)
    low = lane < HEAD_SIZE
    return jnp.concatenate(
        [jnp.where(low, block, zero), jnp.where(low, zero, block)], axis=0
    )


def allowed_pairs(seg_row, seg_column):
    length = seg_column.shape[0]
    rows = lax.broadcasted_iota(jnp.int32, (length, length), 0)
    columns = lax.broadcasted_iota(jnp.int32, (length, length), 1)
    allowed = (columns <= rows) & (seg_column == seg_row)
    bias = jnp.where(allowed, 0.0, 1.0)
    return jnp.concatenate([bias, bias], axis=0) < 0.5


def store_blocks(keep_ref, send_ref, value, column, width, stream, my_core, my_place):
    rows = value.shape[0] // 64
    for block in range(32):
        x, yh, z = block // 8, (block // 4) % 2, block % 4
        at = place(stream, x, yh, z)
        to = pl.multiple_of((my_place ^ at) * rows, rows)
        first = value[2 * block * rows : (2 * block + 1) * rows]
        second = value[(2 * block + 1) * rows : (2 * block + 2) * rows]
        keep_ref[pl.ds(to, rows), column : column + width] = jnp.where(
            my_core == 0, first, second
        )
        send_ref[pl.ds(to, rows), column : column + width] = jnp.where(
            my_core == 0, second, first
        )


def store_natural(keep_ref, send_ref, value, column, width, my_core):
    rows = value.shape[0] // 64
    for block in range(32):
        first = value[2 * block * rows : (2 * block + 1) * rows]
        second = value[(2 * block + 1) * rows : (2 * block + 2) * rows]
        at = slice(block * rows, (block + 1) * rows)
        keep_ref[at, column : column + width] = jnp.where(my_core == 0, first, second)
        send_ref[at, column : column + width] = jnp.where(my_core == 0, second, first)


def attention_forward_kernel(count, *refs):
    parts = refs[:count]
    (gain, wq, wk, wv, wo, cos, sin, seg_row, seg_column) = refs[count : count + 9]
    (x_out, a_out, q_out, kk_out, vv_out, mix_out, part_out) = refs[count + 9 :]
    x = parts[0][...].astype(F32)
    if count == 3:
        x = x + (parts[1][...] + parts[2][...])
    x_out[...] = x
    length = x.shape[0]
    a = (x * row_factor(x) * gain[...].astype(F32)).astype(BF16)
    a_out[...] = a
    lane = lane_of(length)
    cosine, sine = cos[...], sin[...]
    q = mm(a, wq[...])
    k = mm(a, wk[...])
    v = mm(a, wv[...])
    allowed = allowed_pairs(seg_row[...], seg_column[...])
    scale = HEAD_SIZE**-0.5
    pairs = k.shape[1] // LANES
    for pair in range(pairs):
        at = slice(pair * LANES, (pair + 1) * LANES)
        k_block = k[:, at] * cosine + partner(k[:, at], lane) * sine
        k_twice = both_heads(k_block, lane)
        v_twice = both_heads(v[:, at], lane)
        for side in range(2):
            head = 2 * pair + side
            columns = slice(head * LANES, (head + 1) * LANES)
            kk = k_twice[side].astype(BF16)
            vv = v_twice[side].astype(BF16)
            kk_out[head] = kk
            vv_out[head] = vv
            q_block = q[:, columns]
            q_block = (q_block * cosine + partner(q_block, lane) * sine).astype(BF16)
            q_out[:, columns] = q_block
            scores = mm_nt(stacked_pair(q_block, lane), kk) * scale
            scores = jnp.where(allowed, scores, EXCLUDED)
            shifted = jnp.exp(scores - jnp.max(scores, axis=-1, keepdims=True))
            probs = (shifted / jnp.sum(shifted, axis=-1, keepdims=True)).astype(BF16)
            mixed = mm(probs, vv)
            mix_out[:, columns] = jnp.where(
                lane < HEAD_SIZE, mixed[:length], mixed[length:]
            ).astype(BF16)
    part_out[...] = mm(mix_out[...], wo[...])


def whole(shape):
    return pl.BlockSpec(shape, lambda i: (0,) * len(shape))


def of_layer(layer, shape):
    return pl.BlockSpec((None, *shape), lambda i: (layer,) + (0,) * len(shape))


def params(mib):
    return pltpu.CompilerParams(
        vmem_limit_bytes=mib * MIB, dimension_semantics=("arbitrary",)
    )


def cost(flops, nbytes):
    return pl.CostEstimate(flops=flops, bytes_accessed=nbytes, transcendentals=0)


def attention_forward(layer, parts, weights, tables, segment):
    gain, wq, wk, wv, wo = weights
    length, features = parts[0].shape
    q_width, k_width = wq.shape[2], wk.shape[2]
    heads = 2 * k_width // LANES
    ins = [*parts, gain, wq, wk, wv, wo, *tables, *segment]
    in_specs = [whole(part.shape) for part in parts]
    in_specs += [of_layer(layer, w.shape[1:]) for w in (gain, wq, wk, wv, wo)]
    in_specs += [whole(t.shape) for t in (*tables, *segment)]
    outs = [
        ((length, features), F32),
        ((length, features), BF16),
        ((length, q_width), BF16),
        ((heads, length, LANES), BF16),
        ((heads, length, LANES), BF16),
        ((length, q_width), BF16),
        ((length, features), F32),
    ]
    return pl.pallas_call(
        functools.partial(attention_forward_kernel, len(parts)),
        grid=(1,),
        in_specs=in_specs,
        out_specs=[whole(shape) for shape, _ in outs],
        out_shape=[jax.ShapeDtypeStruct(*out) for out in outs],
        compiler_params=params(48),
        cost_estimate=cost(1 << 30, 8 * MIB),
        name="attention_forward",
    )(*ins)


def column_of(table, lane, index):
    return jnp.sum(jnp.where(lane == index, table, 0.0), axis=1, keepdims=True)


def expert_prologue(x, own, other, gain, router, mask, middle_out, xi_out, share_out):
    middle = x[...] + (own[...] + other[...])
    middle_out[...] = middle
    xi = (middle * row_factor(middle) * gain[...].astype(F32)).astype(BF16)
    xi_out[...] = xi
    logits = mm(xi, router[...])
    chosen = mask[...] > 0.5
    logits = jnp.where(chosen, logits, EXCLUDED)
    shifted = jnp.exp(logits - jnp.max(logits, axis=-1, keepdims=True))
    shifted = jnp.where(chosen, shifted, 0.0)
    share_out[...] = shifted / jnp.sum(shifted, axis=-1, keepdims=True)


def expert_step(gate_in, linear, wd, share):
    squashed = 1.0 / (1.0 + jnp.exp(-gate_in))
    silu = gate_in * squashed
    activation = (silu * linear).astype(BF16)
    return squashed, silu, activation, mm(activation, wd)


def expert_backward_step(
    stream, places, g, xi, share, gate_in, linear, wg, wu, wd, keep, send, natural
):
    my_core, my_place = places
    squashed, silu, activation, expert_out = expert_step(gate_in, linear, wd, share)
    gate_grad = jnp.sum(g * expert_out, axis=1, keepdims=True)
    expert_grad = (share * g).astype(BF16)
    activation_grad = mm_nt(expert_grad, wd)
    gate_in_grad = (
        activation_grad * linear * squashed * (1.0 + gate_in * (1.0 - squashed))
    ).astype(BF16)
    linear_grad = (activation_grad * silu).astype(BF16)
    width = activation.shape[1]

    def store(value, column):
        if natural:
            store_natural(keep, send, value, column, width, my_core)
        else:
            store_blocks(keep, send, value, column, width, stream, my_core, my_place)

    store(mm_tn(xi, gate_in_grad), 0)
    store(mm_tn(xi, linear_grad), width)
    store(mm_tn(expert_grad, activation), 2 * width)
    return gate_grad, mm_nt(gate_in_grad, wg) + mm_nt(linear_grad, wu), expert_out


def expert_forward_kernel(
    x, own, other, gain, router, mask, wg, wu, wd,
    middle_out, xi_out, share_out, gate_out, linear_out, part_out,
):
    expert = pl.program_id(0)

    @pl.when(expert == 0)
    def _():
        expert_prologue(x, own, other, gain, router, mask, middle_out, xi_out, share_out)
        part_out[...] = jnp.zeros_like(part_out)

    share = column_of(share_out[...], lane_of(share_out.shape[0]), expert)
    xi = xi_out[...]
    gate_in = mm(xi, wg[...])
    linear = mm(xi, wu[...])
    gate_out[...] = gate_in
    linear_out[...] = linear
    part_out[...] += share * expert_step(gate_in, linear, wd[...], share)[3]


def expert_both_kernel(
    places, x, own, other, gain, router, mask, wg, wu, wd, cotangent,
    middle_out, xi_out, share_out, part_out, back_out, gate_grad_out, keep, send,
):
    expert = pl.program_id(0)
    lane = lane_of(share_out.shape[0])

    @pl.when(expert == 0)
    def _():
        expert_prologue(x, own, other, gain, router, mask, middle_out, xi_out, share_out)
        part_out[...] = jnp.zeros_like(part_out)
        back_out[...] = jnp.zeros_like(back_out)
        gate_grad_out[...] = jnp.zeros_like(gate_grad_out)

    share = column_of(share_out[...], lane, expert)
    xi = xi_out[...]
    gate_in = mm(xi, wg[...])
    linear = mm(xi, wu[...])
    gate_grad, back, expert_out = expert_backward_step(
        0, (places[STREAMS], 0), cotangent[...].astype(F32), xi, share,
        gate_in, linear, wg[...], wu[...], wd[...], keep, send, True,
    )
    part_out[...] += share * expert_out
    back_out[...] += back
    gate_grad_out[...] += jnp.where(lane == expert, gate_grad, 0.0)


def expert_backward_kernel(
    places, g_in, x, gain, own, other, xi_ref, share_ref, gate_ref, linear_ref, wg, wu, wd,
    g_out, gain_out, back_out, gate_grad_out, keep, send,
):
    expert = pl.program_id(0)
    lane = lane_of(share_ref.shape[0])

    @pl.when(expert == 0)
    def _():
        stream = x[...]
        change, gain_row = norm_back(
            stream, row_factor(stream), gain[...].astype(F32), own[...] + other[...]
        )
        g_out[...] = g_in[...] + change
        gain_out[...] = jnp.broadcast_to(gain_row, gain_out.shape)
        back_out[...] = jnp.zeros_like(back_out)
        gate_grad_out[...] = jnp.zeros_like(gate_grad_out)

    def stored_for(stream):
        @pl.when(expert == stream)
        def _():
            share = column_of(share_ref[...], lane, stream)
            gate_grad, back, _ = expert_backward_step(
                stream, (places[STREAMS], places[stream]), g_out[...], xi_ref[...], share,
                gate_ref[...], linear_ref[...], wg[...], wu[...], wd[...], keep, send, False,
            )
            back_out[...] += back
            gate_grad_out[...] += jnp.where(lane == stream, gate_grad, 0.0)

    for stream in range(STREAMS):
        stored_for(stream)


def of_expert(layer, shape):
    return pl.BlockSpec((None, None, *shape), lambda e: (layer, e, 0, 0))


def each_expert(shape):
    return pl.BlockSpec((None, *shape), lambda e: (e, 0, 0))


def gradient_outs(rows, width):
    spec = pl.BlockSpec((rows, 3 * width), lambda e: (0, e))
    shape = ((rows, 3 * width * STREAMS), F32)
    return [(spec, shape)] * 2


SMEM = pl.BlockSpec(memory_space=pltpu.SMEM)


def run_experts(kernel, name, ins, in_specs, outs, flops, nbytes, mib):
    return pl.pallas_call(
        kernel,
        grid=(STREAMS,),
        in_specs=in_specs,
        out_specs=[spec for spec, _ in outs],
        out_shape=[jax.ShapeDtypeStruct(*out) for _, out in outs],
        compiler_params=params(mib),
        cost_estimate=cost(flops, nbytes),
        name=name,
    )(*ins)


def expert_forward(layer, x, own, other, gain, router, mask, wg, wu, wd):
    length, features = x.shape
    width = wg.shape[3]
    big, low = ((length, features), F32), ((length, features), BF16)
    hidden = (each_expert((length, width)), ((STREAMS, length, width), F32))
    ins = [x, own, other, gain, router, mask, wg, wu, wd]
    in_specs = [whole(x.shape)] * 3 + [
        of_layer(layer, gain.shape[1:]),
        of_layer(layer, router.shape[1:]),
        of_layer(layer, mask.shape[1:]),
        *(of_expert(layer, w.shape[2:]) for w in (wg, wu, wd)),
    ]
    outs = [
        (whole(big[0]), big),
        (whole(low[0]), low),
        (whole((length, LANES)), ((length, LANES), F32)),
        hidden,
        hidden,
        (whole(big[0]), big),
    ]
    return run_experts(
        expert_forward_kernel, "experts_forward", ins, in_specs, outs, 8 << 28, 12 * MIB, 48
    )


def expert_both(layer, places, x, own, other, gain, router, mask, wg, wu, wd, cotangent):
    length, features = x.shape
    width = wg.shape[3]
    big, low = ((length, features), F32), ((length, features), BF16)
    table = (whole((length, LANES)), ((length, LANES), F32))
    ins = [places, x, own, other, gain, router, mask, wg, wu, wd, cotangent]
    in_specs = [SMEM] + [whole(x.shape)] * 3 + [
        of_layer(layer, gain.shape[1:]),
        of_layer(layer, router.shape[1:]),
        of_layer(layer, mask.shape[1:]),
        *(of_expert(layer, w.shape[2:]) for w in (wg, wu, wd)),
        whole(cotangent.shape),
    ]
    outs = [
        (whole(big[0]), big),
        (whole(low[0]), low),
        table,
        (whole(big[0]), big),
        (whole(big[0]), big),
        table,
        *gradient_outs(features // 2, width),
    ]
    return run_experts(
        expert_both_kernel, "experts_both", ins, in_specs, outs, 5 << 30, 30 * MIB, 56
    )


def expert_backward(layer, places, g, x, gain, own, other, xi, share, gate_in, linear, wg, wu, wd):
    length, features = x.shape
    width = wg.shape[3]
    big = ((length, features), F32)
    table = (whole((length, LANES)), ((length, LANES), F32))
    hidden = each_expert((length, width))
    ins = [places, g, x, gain, own, other, xi, share, gate_in, linear, wg, wu, wd]
    in_specs = [SMEM, whole(x.shape), whole(x.shape)] + [
        of_layer(layer + 1, gain.shape[1:]),
        whole(x.shape),
        whole(x.shape),
        whole(x.shape),
        whole(share.shape),
        hidden,
        hidden,
        *(of_expert(layer, w.shape[2:]) for w in (wg, wu, wd)),
    ]
    outs = [
        (whole(big[0]), big),
        (whole((8, features)), ((8, features), F32)),
        (whole(big[0]), big),
        table,
        *gradient_outs(features // 2, width),
    ]
    return run_experts(
        expert_backward_kernel, "experts_backward", ins, in_specs, outs, 4 << 30, 30 * MIB, 56
    )


def stream_columns(stream, width):
    return SMALL + width * stream if stream else 0


def attention_backward_kernel(
    places, g, own, other, gate_own, gate_other, middle, xi, share, gain, router_rows,
    wo, mix, q, kk, vv, a, wq, wk, wv, cos, sin, seg_row, seg_column, x, late_gain,
    g_out, part_out, keep, send, rows_scratch,
):
    my_core = places[STREAMS]
    length = middle.shape[0]
    lane = lane_of(length)
    shares = share[...]
    gate_grad = gate_own[...] + gate_other[...]
    pick = shares * (gate_grad - jnp.sum(shares * gate_grad, axis=1, keepdims=True))
    input_grad = own[...] + other[...]
    xi_full = xi[...].astype(F32)
    rows_scratch[...] = jnp.zeros_like(rows_scratch)
    for expert in range(STREAMS):
        logit_grad = column_of(pick, lane, expert)
        input_grad = input_grad + logit_grad * router_rows[expert : expert + 1, :]
        rows_scratch[expert : expert + 1, :] = jnp.sum(
            xi_full * logit_grad, axis=0, keepdims=True
        )
    mid = middle[...]
    change, gain_row = norm_back(mid, row_factor(mid), gain[...].astype(F32), input_grad)
    rows_scratch[4:5, :] = gain_row
    rows_scratch[6:7, :] = late_gain[0:1, :]
    gradient = g[...].astype(F32) + change
    g_out[...] = gradient
    output_grad = gradient.astype(BF16)
    mixture_grad = mm_nt(output_grad, wo[...]).astype(BF16)

    part = q.shape[1] // LANES
    gradients = [None] * (3 * part)
    projection = mm_tn(output_grad, mix[...])
    cosine, sine = cos[...], sin[...]
    allowed = allowed_pairs(seg_row[...], seg_column[...])
    scale = HEAD_SIZE**-0.5
    low = lane < HEAD_SIZE
    a_full = a[...]
    query_grads, key_grads, value_grads = [], [], []
    for pair in range(part // 2):
        key_sides, value_sides = [], []
        for side in range(2):
            head = 2 * pair + side
            columns = slice(head * LANES, (head + 1) * LANES)
            stacked = stacked_pair(q[:, columns], lane)
            scores = jnp.where(allowed, mm_nt(stacked, kk[head]) * scale, EXCLUDED)
            shifted = jnp.exp(scores - jnp.max(scores, axis=-1, keepdims=True))
            probs = shifted / jnp.sum(shifted, axis=-1, keepdims=True)
            mix_grad = stacked_pair(mixture_grad[:, columns], lane)
            prob_grad = mm_nt(mix_grad, vv[head])
            inner = jnp.sum(probs * prob_grad, axis=-1, keepdims=True)
            score_grad = (probs * (prob_grad - inner)).astype(BF16)
            query = mm(score_grad, kk[head])
            query = jnp.where(low, query[:length], query[length:]) * scale
            query = query * cosine - partner(query, lane) * sine
            query_grads.append(query.astype(BF16))
            key = mm_tn(score_grad, stacked) * scale
            key_sides.append(key + pltpu.roll(key, HEAD_SIZE, 1))
            value = mm_tn(probs.astype(BF16), mix_grad)
            value_sides.append(value + pltpu.roll(value, HEAD_SIZE, 1))
        key = jnp.where(low, key_sides[0], key_sides[1])
        key_grads.append((key * cosine - partner(key, lane) * sine).astype(BF16))
        value_grads.append(jnp.where(low, value_sides[0], value_sides[1]).astype(BF16))
    query_grad = jnp.concatenate(query_grads, axis=1)
    key_grad = jnp.concatenate(key_grads, axis=1)
    value_grad = jnp.concatenate(value_grads, axis=1)
    attention_part = (
        mm_nt(query_grad, wq[...]) + mm_nt(key_grad, wk[...]) + mm_nt(value_grad, wv[...])
    )
    part_out[...] = attention_part
    stream = x[...]
    rows_scratch[5:6, :] = jnp.sum(
        attention_part * stream * row_factor(stream), axis=0, keepdims=True
    )

    totals = [mm_tn(a_full, query_grad), mm_tn(a_full, key_grad), mm_tn(a_full, value_grad)]
    totals.append(projection)
    pieces = [total[:, at : at + LANES] for total in totals for at in range(0, total.shape[1], LANES)]
    small = jnp.transpose(rows_scratch[...])
    per_stream = len(pieces) // STREAMS
    for stream_index in range(STREAMS):
        column = stream_columns(stream_index, per_stream * LANES)
        mine = pieces[stream_index * per_stream : (stream_index + 1) * per_stream]
        if stream_index == 0:
            mine = [small] + mine
        for piece in mine:
            store_blocks(
                keep, send, piece, column, LANES, stream_index, my_core, places[stream_index]
            )
            column += LANES


def attention_backward(
    layer, places, g, own, other, gate_own, gate_other, saved_experts, weights, saved, tables,
    segment, late_gain,
):
    middle, xi, share = saved_experts
    gain, router_rows, wo, wq, wk, wv = weights
    x, a, q, kk, vv, mix = saved
    length, features = middle.shape
    columns = SMALL + wq.shape[2] + wk.shape[2] + wv.shape[2] + wo.shape[1]
    ins = [
        places, g, own, other, gate_own, gate_other, middle, xi, share, gain, router_rows,
        wo, mix, q, kk, vv, a, wq, wk, wv, *tables, *segment, x, late_gain,
    ]
    layered = {9, 10, 11, 17, 18, 19}
    in_specs = [SMEM]
    for at, array in enumerate(ins[1:], 1):
        in_specs.append(of_layer(layer, array.shape[1:]) if at in layered else whole(array.shape))
    outs = [
        ((length, features), F32),
        ((length, features), F32),
        ((features // 2, columns), F32),
        ((features // 2, columns), F32),
    ]
    return pl.pallas_call(
        attention_backward_kernel,
        grid=(1,),
        in_specs=in_specs,
        out_specs=[whole(shape) for shape, _ in outs],
        out_shape=[jax.ShapeDtypeStruct(*out) for out in outs],
        scratch_shapes=[pltpu.VMEM((LANES, features), F32)],
        compiler_params=params(56),
        cost_estimate=cost(3 << 30, 18 * MIB),
        name="attention_backward",
    )(*ins)


SWAP = ((0, 1), (1, 0))
RING = {"u": tuple((i, i ^ 1) for i in range(4)), "v": tuple((i, 3 - i) for i in range(4))}


def exchange(array):
    return lax.ppermute(array, "tensor", SWAP)


def scatter_streams(keep, send, columns):
    received = lax.ppermute(send, "dp_3", SWAP)
    streams = [
        (keep[:, start : start + width], received[:, start : start + width])
        for start, width in columns
    ]
    for step in range(4):
        half = 256 >> step
        sends = [first[half:] + second[half:] for first, second in streams]
        moved = []
        for stream, block in enumerate(sends):
            ring, kind = ORDERS[stream][step]
            moved.append(lax.ppermute(block, "dp_0" if ring == "x" else "dp_2", RING[kind]))
        streams = [
            (first[:half] + second[:half], block)
            for (first, second), block in zip(streams, moved)
        ]
    summed = [first + second for first, second in streams]
    packed = jnp.concatenate(summed, axis=1)
    half = packed.shape[0] // 2
    packed = packed[:half] + lax.ppermute(packed[half:], "dp_1", SWAP)
    starts = np.cumsum([0] + [width for _, width in columns])
    return [packed[:, a:b] for a, b in zip(starts[:-1], starts[1:])]


def scatter_natural(keep, send):
    summed = keep + lax.ppermute(send, "dp_3", SWAP)
    return lax.psum_scatter(
        summed, ("dp_0", "dp_1", "dp_2"), scatter_dimension=0, tiled=True
    )


def rope_tables(length):
    half = HEAD_SIZE // 2
    frequency = np.float32(THETA) ** (-2.0 * np.arange(half, dtype=np.float32) / HEAD_SIZE)
    angles = np.arange(length, dtype=np.float32)[:, None] * frequency[None].astype(np.float32)
    angles = angles.astype(np.float32)
    cosine = np.tile(np.cos(angles), (1, LANES // half)).astype(np.float32)
    sine = np.sin(angles)
    sine = np.tile(np.concatenate([-sine, sine], axis=1), (1, LANES // HEAD_SIZE))
    return jnp.asarray(cosine), jnp.asarray(sine.astype(np.float32))


def shards(
    tokens, segments, routes, norm_attention, query_weight, key_matrix, value_matrix,
    output_weight, norm_experts, router_weight, gate_weight, up_weight, down_weight, cotangent,
):
    length, features = tokens.shape
    experts = gate_weight.shape[1]
    hidden = gate_weight.shape[3]
    tables = rope_tables(length)
    segment = (segments.reshape(1, length), segments.reshape(length, 1))
    gain_attention = norm_attention[:, None, :]
    gain_experts = norm_experts[:, None, :]
    router = jnp.pad(router_weight, ((0, 0), (0, 0), (0, LANES - experts)))
    router_rows = jnp.pad(
        jnp.swapaxes(router_weight, 1, 2).astype(F32), ((0, 0), (0, 8 - experts), (0, 0))
    )
    mask = jnp.any(
        routes[..., None] == jnp.arange(LANES, dtype=jnp.int32), axis=2
    ).astype(F32)
    x_at, y_at, z_at = (lax.axis_index(name) for name in DP[:3])
    places = jnp.stack(
        [place(stream, x_at, y_at, z_at) for stream in range(STREAMS)]
        + [lax.axis_index("dp_3")]
    ).astype(jnp.int32)

    attention_weights = (gain_attention, query_weight, key_matrix, value_matrix, output_weight)
    expert_weights = (gate_weight, up_weight, down_weight)
    back_weights = (
        gain_experts, router_rows, output_weight, query_weight, key_matrix, value_matrix,
    )

    x1, *saved1, part = attention_forward(0, [tokens], attention_weights, tables, segment)
    middle1, xi1, share1, gate1, linear1, part = expert_forward(
        0, x1, part, exchange(part), gain_experts, router, mask, *expert_weights
    )
    x2, *saved2, part = attention_forward(
        1, [middle1, part, exchange(part)], attention_weights, tables, segment
    )
    middle2, xi2, share2, last, back, gate_grad, keep_e2, send_e2 = expert_both(
        1, places, x2, part, exchange(part), gain_experts, router, mask, *expert_weights, cotangent
    )
    no_gain = jnp.zeros((8, features), F32)
    g2, part, keep_a2, send_a2 = attention_backward(
        1, places, cotangent, back, exchange(back), gate_grad, exchange(gate_grad),
        (middle2, xi2, share2), back_weights, (x2, *saved2), tables, segment, no_gain,
    )
    g1, late_gain, back, gate_grad, keep_e1, send_e1 = expert_backward(
        0, places, g2, x2, gain_attention, part, exchange(part), xi1, share1, gate1, linear1,
        *expert_weights,
    )
    g0, part, keep_a1, send_a1 = attention_backward(
        0, places, g1, back, exchange(back), gate_grad, exchange(gate_grad),
        (middle1, xi1, share1), back_weights, (x1, *saved1), tables, segment, late_gain,
    )
    gain = norm_attention[0].astype(F32)
    change, _ = norm_back(x1, row_factor(x1), gain, part + exchange(part))
    gradient = g0 + change
    output = (middle2 + (last + exchange(last))).astype(BF16)

    width = (query_weight.shape[2] + 2 * key_matrix.shape[2] + output_weight.shape[1]) // STREAMS
    attention_columns = [
        (stream_columns(s, width), width + (0 if s else SMALL)) for s in range(STREAMS)
    ]
    expert_columns = [(s * 3 * hidden, 3 * hidden) for s in range(STREAMS)]
    block_e2 = scatter_natural(keep_e2, send_e2)
    blocks_a2 = scatter_streams(keep_a2, send_a2, attention_columns)
    blocks_e1 = scatter_streams(keep_e1, send_e1, expert_columns)
    blocks_a1 = scatter_streams(keep_a1, send_a1, attention_columns)

    def split_attention(blocks):
        whole_row = jnp.concatenate(blocks, axis=1)
        bounds = np.cumsum(
            [0, SMALL, query_weight.shape[2], key_matrix.shape[2], value_matrix.shape[2],
             output_weight.shape[1]]
        )
        return [whole_row[:, a:b] for a, b in zip(bounds[:-1], bounds[1:])]

    def split_experts(block):
        block = block.reshape(block.shape[0], experts, 3, hidden)
        return [jnp.swapaxes(block[:, :, kind], 0, 1) for kind in range(3)]

    attention_sums = [split_attention(blocks) for blocks in (blocks_a1, blocks_a2)]
    expert_sums = [split_experts(jnp.concatenate(blocks_e1, axis=1)), split_experts(block_e2)]
    small = jnp.stack([sums[0] for sums in attention_sums])
    attention_gain = small[:, :, 5]
    attention_gain = attention_gain + exchange(attention_gain)
    return (
        output,
        gradient,
        attention_gain,
        *(jnp.stack([sums[at] for sums in attention_sums]) for at in (1, 2, 3)),
        jnp.swapaxes(jnp.stack([sums[4] for sums in attention_sums]), 1, 2),
        small[:, :, 4],
        small[:, :, :experts],
        *(jnp.stack([sums[kind] for sums in expert_sums]) for kind in (0, 1)),
        jnp.swapaxes(jnp.stack([sums[2] for sums in expert_sums]), 2, 3),
    )


def solution(mesh):
    torus = Mesh(
        mesh.devices.reshape(*DP_SIZES, mesh.shape["tensor"]), (*DP, "tensor")
    )
    rows, copied, last = P(DP, None), P(), P(None, None, "tensor")
    in_specs = (
        rows, rows, P(None, DP, None), copied, last, last, last, P(None, "tensor", None),
        copied, copied, P(None, None, None, "tensor"), P(None, None, None, "tensor"),
        P(None, None, "tensor", None), rows,
    )
    out_specs = (
        rows, rows, P(None, DP), P(None, DP, "tensor"), P(None, DP, "tensor"),
        P(None, DP, "tensor"), P(None, "tensor", DP), P(None, DP), P(None, DP, None),
        P(None, None, DP, "tensor"), P(None, None, DP, "tensor"), P(None, None, "tensor", DP),
    )
    return jax.shard_map(
        shards, mesh=torus, in_specs=in_specs, out_specs=out_specs, check_vma=False
    )
```

time: 1340 us -> 608 us (0.45)
  local copies, waits for them, and re-layouts: 410 us -> 28.7 us
  matrix products: 320 us -> 0 us
  Pallas kernels: 0 us -> 75.5 us
  other arithmetic: 92.5 us -> 20.3 us
  loops' own time: 62.4 us -> 0 us
  starting transfers between devices: 28.8 us -> 89.3 us
  blocking collectives: 40.4 us -> 0 us
  waiting for transfers between devices: 354 us -> 370 us
    dot_general x186 -> x0, matrix products: 320 us -> none  [the longest x16 37.3 us: one_block(): jnp.einsum('rf,rd->fd', active_block, incoming, preferred_element_type=jn...]
    ppermute x0 -> x66, waiting for transfers between devices: none -> 250 us  [the longest x11 153 us: exchange(): return lax.ppermute(array, 'tensor', SWAP)]
    reduce_scatter x2 -> x1, waiting for transfers between devices: 289 us -> 121 us  [scatter_natural(): lax.psum_scatter(summed, ('dp_0', 'dp_1', 'dp_2'), scatter_dimension=0, t...]
    concatenate x16 -> x0, local copies, waits for them, and re-layouts: 106 us -> none  [the longest x12 106 us: pack_major(): return jnp.concatenate(flattened, axis=1)]
    ppermute x0 -> x66, starting transfers between devices: none -> 89.2 us  [the longest x48 66.6 us: scatter_streams(): lax.ppermute(block, 'dp_0' if ring == 'x' else 'dp_2', RING[kind])]
    transpose x9 -> x0, local copies, waits for them, and re-layouts: 78.5 us -> none  [the longest x7 51.4 us: pack_major(): jnp.moveaxis(member, position, 0).reshape(member.shape[position], -1)]
    pallas_call x0 -> x7, Pallas kernels: none -> 75.5 us  [the longest x3 34.6 us: run_experts(): pl.pallas_call(kernel, grid=(STREAMS,), in_specs=in_specs, out_specs=[spe...]
    dynamic_slice x64 -> x0, local copies, waits for them, and re-layouts: 67 us -> none  [the longest x32 48.1 us: add_at(): current = lax.dynamic_index_in_dim(totals, index_value, 0, keepdims=False)]
  transfers between devices with their start and end apart: 10 -> 67, of which waited for: 7 -> 42; matrix products, arithmetic and copies ran while one was open for 14% -> 4% of each run, Pallas kernels for 0% -> 5%
where the time goes in v1:
time: 608 us; the launch traced here: 599 us
  waiting for transfers between devices  370 us (61%)
  starting transfers between devices  89.3 us (15%)
  Pallas kernels  75.5 us (12%)
  local copies, waits for them, and re-layouts  28.7 us (5%)
  other arithmetic  20.3 us (3%)
  between operations  15.3 us (3%)
    ppermute x11, waiting for transfers between devices, exchange(): return lax.ppermute(array, 'tensor', SWAP)  153 us
    reduce_scatter x1, waiting for transfers between devices, scatter_natural(): lax.psum_scatter(summed, ('dp_0', 'dp_1', 'dp_2'), scatter_dimension=0, t...  121 us
    ppermute x48, waiting for transfers between devices, scatter_streams(): lax.ppermute(block, 'dp_0' if ring == 'x' else 'dp_2', RING[kind])  87.7 us
    ppermute x48, starting transfers between devices, scatter_streams(): lax.ppermute(block, 'dp_0' if ring == 'x' else 'dp_2', RING[kind])  66.6 us
    pallas_call x3, Pallas kernels, run_experts(): pl.pallas_call(kernel, grid=(STREAMS,), in_specs=in_specs, out_specs=[spe...  34.6 us
    pallas_call x2, Pallas kernels, attention_backward(): pl.pallas_call(attention_backward_kernel, grid=(1,), in_specs=in_specs, o...  29.7 us
    unnamed x117, local copies, waits for them, and re-layouts  23.5 us
    ppermute x11, starting transfers between devices, exchange(): return lax.ppermute(array, 'tensor', SWAP)  16.1 us
  transfers between devices with their start and end apart: 67, of which 42 were waited for; matrix products, arithmetic and copies ran while one was open for 4% of the time, Pallas kernels for 5%

profile of v1, /device:TPU:0, one launch (start us, length us, event | category | flops | bytes accessed | tf_op | source)
XLA Modules:
  0.0 599.4 jit_solution(11415667962221227077)
XLA Ops:
  13.5 5.3 attention_forward.2
  25.1 22.5 %collective-permute-done.other = f32[256,1024]{1,0:T(8,128)} collective-permute-done((f32[256,1024]{1,0:T(8,128)S(1)}, f32[256,1024]{1,0:T(8,128)}, u32[]{:S(2)}, u32[]{:S(2)}) %collective-permute-start) | collective-permute-done | bytes 1048608 | tf_op jit(solution)/shard_map/ppermute | solution.py:599
  47.6 6.8 %experts_forward.1 = (f32[256,1024]{1,0:T(8,128)S(1)}, bf16[256,1024]{1,0:T(8,128)(2,1)S(1)}, f32[256,128]{1,0:T(8,128)S(1)}, f32[4,256,256]{2,1,0:T(8,128)S(1)}...) custom-call(f32[256,1024]{1,0:T(8,128)} %copy-done.1, f32[256,1024]{1,0:T(8,128)} %copy-done.13, ...), custom_call_target="tpu_custom_call" | custom-call | flops 2147483648 | bytes 12582912 | tf_op jit(solution)/shard_map/experts_forward/pallas_call | solution.py:370
  56.3 1.7 collective-permute-start.1
  58.1 22.3 %collective-permute-done.1.refs_2_ = f32[256,1024]{1,0:T(8,128)S(1)} collective-permute-done((f32[256,1024]{1,0:T(8,128)S(1)}, f32[256,1024]{1,0:T(8,128)S(1)}, u32[]{:S(2)}, u32[]{:S(2)}) %collective-permute-start.1) | collective-permute-done | bytes 1048608 | tf_op jit(solution)/shard_map/ppermute | solution.py:599
  81.4 5.8 attention_forward.3
  94.2 20.8 %collective-permute-done.2.other = f32[256,1024]{1,0:T(8,128)S(1)} collective-permute-done((f32[256,1024]{1,0:T(8,128)S(1)}, f32[256,1024]{1,0:T(8,128)S(1)}, u32[]{:S(2)}, u32[]{:S(2)}) %collective-permute-start.2) | collective-permute-done | bytes 1048608 | tf_op jit(solution)/shard_map/ppermute | solution.py:599
  115.9 13.6 %experts_both.1 = (f32[256,1024]{1,0:T(8,128)}, bf16[256,1024]{1,0:T(8,128)(2,1)}, f32[256,128]{1,0:T(8,128)}, f32[256,1024]{1,0:T(8,128)}, f32[256,1024]{1,0:T(...) custom-call(s32[5]{0:T(128)} %stack.95.places, f32[256,1024]{1,0:T(8,128)} %copy-done.4, ...), custom_call_target="tpu_custom_call" | custom-call | flops 5368709120 | bytes 31457280 | tf_op jit(solution)/shard_map/experts_both/pallas_call | solution.py:370
  129.5 1.8 collective-permute-start.4
  132.4 22.3 %collective-permute-done.5.gate_other = f32[256,128]{1,0:T(8,128)S(1)} collective-permute-done((f32[256,128]{1,0:T(8,128)}, f32[256,128]{1,0:T(8,128)S(1)}, u32[]{:S(2)}, u32[]{:S(2)}) %collective-permute-start.5) | collective-permute-done | bytes 131104 | tf_op jit(solution)/shard_map/ppermute | solution.py:599
  155.8 14.7 %attention_backward.2 = (f32[256,1024]{1,0:T(8,128)}, f32[256,1024]{1,0:T(8,128)}, f32[512,1664]{1,0:T(8,128)}, f32[512,1664]{1,0:T(8,128)}) custom-call(s32[5]{0:T(128)} %stack.95.places, bf16[256,1024]{1,0:T(8,128)(2,1)} %g.1, f32[256,1024]{1,0:T(8,128)} %get-tuple-element.62.own, f32[256,1024]{1,0:T(8,128)} %copy-done.38, ...), custom_call_target="tpu_custom_call" | custom-call | flops 3221225472 | bytes 18874368 | tf_op jit(solution)/shard_map/attention_backward/pallas_call | solution.py:581
  170.5 1.8 collective-permute-start.6
  172.7 19.3 %collective-permute-done.6.other = f32[256,1024]{1,0:T(8,128)S(1)} collective-permute-done((f32[256,1024]{1,0:T(8,128)}, f32[256,1024]{1,0:T(8,128)S(1)}, u32[]{:S(2)}, u32[]{:S(2)}) %collective-permute-start.6) | collective-permute-done | bytes 1048608 | tf_op jit(solution)/shard_map/ppermute | solution.py:599
  193.1 14.2 %experts_backward.1 = (f32[256,1024]{1,0:T(8,128)}, f32[8,1024]{1,0:T(8,128)}, f32[256,1024]{1,0:T(8,128)}, f32[256,128]{1,0:T(8,128)}, f32[512,3072]{1,0:T(8,128)}, /*index=5*/f32[512,3072]{1,0:T(8,128)}) custom-call(s32[5]{0:T(128)} %stack.95.places, f32[256,1024]{1,0:T(8,128)} %get-tuple-element.71.g_in, f32[256,1024]{1,0:T(8,128)} %copy-done.4, ...), custom_call_target="tpu_custom_call" | custom-call | flops 4294967296 | bytes 31457280 | tf_op jit(solution)/shard_map/experts_backward/pallas_call | solution.py:370
  207.3 1.8 collective-permute-start.7
  209.5 1.9 collective-permute-start.3
  211.3 25.2 %collective-permute-done.8.gate_other = f32[256,128]{1,0:T(8,128)S(1)} collective-permute-done((f32[256,128]{1,0:T(8,128)}, f32[256,128]{1,0:T(8,128)S(1)}, u32[]{:S(2)}, u32[]{:S(2)}) %collective-permute-start.8) | collective-permute-done | bytes 131104 | tf_op jit(solution)/shard_map/ppermute | solution.py:599
  237.6 15.0 %attention_backward.3 = (f32[256,1024]{1,0:T(8,128)}, f32[256,1024]{1,0:T(8,128)}, f32[512,1664]{1,0:T(8,128)}, f32[512,1664]{1,0:T(8,128)}) custom-call(s32[5]{0:T(128)} %stack.95.places, f32[256,1024]{1,0:T(8,128)} %get-tuple-element.77.g, f32[256,1024]{1,0:T(8,128)} %get-tuple-element.78.own, f32[256,1024]{1,0:T(8,128)} %copy-done.41, ...), custom_call_target="tpu_custom_call" | custom-call | flops 3221225472 | bytes 18874368 | tf_op jit(solution)/shard_map/attention_backward/pallas_call | solution.py:581
  252.6 1.8 collective-permute-start.9
  254.5 4.5 collective-permute-done.3
  260.0 15.6 %collective-permute-done.9 = f32[256,1024]{1,0:T(8,128)S(1)} collective-permute-done((f32[256,1024]{1,0:T(8,128)}, f32[256,1024]{1,0:T(8,128)S(1)}, u32[]{:S(2)}, u32[]{:S(2)}) %collective-permute-start.9) | collective-permute-done | bytes 1048608 | tf_op jit(solution)/shard_map/ppermute | solution.py:599
  276.3 4.3 collective-permute-start.41
  280.5 2.9 collective-permute-start.37
  283.6 2.7 collective-permute-done.41
  291.4 6.2 %collective-permute-done.29 = f32[256,512]{1,0:T(8,128)S(1)} collective-permute-done((f32[256,512]{1,0:T(8,128)S(1)}, f32[256,512]{1,0:T(8,128)S(1)}, u32[]{:S(2)}, u32[]{:S(2)}) %collective-permute-start.29) | collective-permute-done | bytes 524320 | tf_op jit(solution)/shard_map/ppermute | solution.py:614
  297.6 3.2 collective-permute-start.38
  300.9 3.0 collective-permute-start.34
  304.5 3.4 collective-permute-done.34
  308.1 4.6 collective-permute-done.43
  313.5 3.8 collective-permute-done.39
  317.3 2.4 collective-permute-start.35
  319.7 3.4 collective-permute-done.35
  323.1 2.9 collective-permute-start.44
  326.1 2.7 collective-permute-done.44
  328.9 3.9 collective-permute-done.40
  332.8 2.9 collective-permute-start.31
  335.7 3.2 collective-permute-done.31
  339.0 2.2 collective-permute-start.32
  341.2 3.3 collective-permute-done.32
  345.3 3.3 collective-permute-start.45
  349.9 3.8 add.570
  355.7 1.8 slice_add_fusion.31
  357.6 2.2 collective-permute-start.23
  359.8 2.7 collective-permute-start.19
  364.1 4.0 collective-permute-done.23
  371.8 1.9 collective-permute-start.16
  375.1 2.4 collective-permute-start.12
  377.6 2.4 collective-permute-start.25
  380.1 2.4 collective-permute-start.17
  386.4 2.1 collective-permute-start.18
  390.1 5.8 collective-permute-done.13
  396.9 5.6 collective-permute-done.14
  403.0 6.3 %collective-permute-done.27 = f32[16,1664]{1,0:T(8,128)S(1)} collective-permute-done((f32[16,1664]{1,0:T(8,128)S(1)}, f32[16,1664]{1,0:T(8,128)S(1)}, u32[]{:S(2)}, u32[]{:S(2)}) %collective-permute-start.27) | collective-permute-done | bytes 106528 | tf_op jit(solution)/shard_map/ppermute | solution.py:622
  409.3 3.8 slice_add_fusion.7
  416.8 15.5 %collective-permute-done.60 = f32[256,768]{1,0:T(8,128)S(1)} collective-permute-done((f32[256,768]{1,0:T(8,128)S(1)}, f32[256,768]{1,0:T(8,128)S(1)}, u32[]{:S(2)}, u32[]{:S(2)}) %collective-permute-start.60) | collective-permute-done | bytes 786464 | tf_op jit(solution)/shard_map/ppermute | solution.py:614
  432.7 3.1 collective-permute-start.57
  439.2 3.2 collective-permute-done.61
  444.1 1.9 collective-permute-start.58
  446.9 3.1 collective-permute-start.50
  454.1 2.7 collective-permute-start.51
  458.2 1.9 collective-permute-done.51
  460.2 2.6 collective-permute-start.64
  464.6 3.0 collective-permute-done.64
  468.0 120.7 %reduce-scatter.2.cloned.1.call-done = f32[16,3072]{1,0:T(8,128)} async-done(((f32[512,3072]{1,0:T(8,128)}), f32[16,3072]{1,0:T(8,128)}) %reduce-scatter.2.cloned.1.call-update) | async-done | bytes 196624 | tf_op jit(solution)/shard_map/reduce_scatter | solution.py:629
  (295 shorter events, 75.8 us)
Async XLA Ops:
  7.2 581.5 %reduce-scatter.2.cloned.1.call-start = ((), (), s32[]{:S(2)}) async-start(), calls=%async_computation.1 | async-start | bytes 6488064 | tf_op jit(solution)/shard_map/reduce_scatter | solution.py:629
  22.7 24.9 %collective-permute-start = (f32[256,1024]{1,0:T(8,128)S(1)}, f32[256,1024]{1,0:T(8,128)}, u32[]{:S(2)}, u32[]{:S(2)}) collective-permute-start(f32[256,1024]{1,0:T(8,128)S(1)} %get-tuple-element.55.own), channel_id=1, source_target_pairs={{0,1},{1,0},{2,3},{3,2},{4,5},{5,4},{6,7},{7,6},{8,9},{9,8},{10,11... | collective-permute-start | bytes 3145736 | tf_op jit(solution)/shard_map/ppermute | solution.py:599
  56.3 24.0 %collective-permute-start.1 = (f32[256,1024]{1,0:T(8,128)S(1)}, f32[256,1024]{1,0:T(8,128)S(1)}, u32[]{:S(2)}, u32[]{:S(2)}) collective-permute-start(f32[256,1024]{1,0:T(8,128)S(1)} %get-tuple-element.57.refs_1_), channel_id=1, source_target_pairs={{0,1},{1,0},{2,3},{3,2},{4,5},{5,4},{6,7},{7,6},{8,9},{9,8},{10,11... | collective-permute-start | bytes 3145736 | tf_op jit(solution)/shard_map/ppermute | solution.py:599
  91.8 23.1 %collective-permute-start.2 = (f32[256,1024]{1,0:T(8,128)S(1)}, f32[256,1024]{1,0:T(8,128)S(1)}, u32[]{:S(2)}, u32[]{:S(2)}) collective-permute-start(f32[256,1024]{1,0:T(8,128)S(1)} %get-tuple-element.59.own), channel_id=1, source_target_pairs={{0,1},{1,0},{2,3},{3,2},{4,5},{5,4},{6,7},{7,6},{8,9},{9,8},{10,11... | collective-permute-start | bytes 3145736 | tf_op jit(solution)/shard_map/ppermute | solution.py:599
  129.5 25.3 %collective-permute-start.4 = (f32[256,1024]{1,0:T(8,128)}, f32[256,1024]{1,0:T(8,128)S(1)}, u32[]{:S(2)}, u32[]{:S(2)}) collective-permute-start(f32[256,1024]{1,0:T(8,128)} %get-tuple-element.62.own), channel_id=1, source_target_pairs={{0,1},{1,0},{2,3},{3,2},{4,5},{5,4},{6,7},{7,6},{8,9},{9,8},{10,11... | collective-permute-start | bytes 3145736 | tf_op jit(solution)/shard_map/ppermute | solution.py:599
  131.3 23.5 %collective-permute-start.5 = (f32[256,128]{1,0:T(8,128)}, f32[256,128]{1,0:T(8,128)S(1)}, u32[]{:S(2)}, u32[]{:S(2)}) collective-permute-start(f32[256,128]{1,0:T(8,128)} %get-tuple-element.63.gate_own), channel_id=1, source_target_pairs={{0,1},{1,0},{2,3},{3,2},{4,5},{5,4},{6,7},{7,6},{8,9},{9,8},{10,11... | collective-permute-start | bytes 393224 | tf_op jit(solution)/shard_map/ppermute | solution.py:599
  170.5 21.6 %collective-permute-start.6 = (f32[256,1024]{1,0:T(8,128)}, f32[256,1024]{1,0:T(8,128)S(1)}, u32[]{:S(2)}, u32[]{:S(2)}) collective-permute-start(f32[256,1024]{1,0:T(8,128)} %get-tuple-element.72.own), channel_id=1, source_target_pairs={{0,1},{1,0},{2,3},{3,2},{4,5},{5,4},{6,7},{7,6},{8,9},{9,8},{10,11... | collective-permute-start | bytes 3145736 | tf_op jit(solution)/shard_map/ppermute | solution.py:599
  172.3 103.6 %collective-permute-start.28 = (f32[512,1664]{1,0:T(8,128)}, f32[512,1664]{1,0:T(8,128)S(1)}, u32[]{:S(2)}, u32[]{:S(2)}) collective-permute-start(f32[512,1664]{1,0:T(8,128)} %get-tuple-element.91), channel_id=1, source_target_pairs={{0,2},{2,0},{1,3},{3,1},{4,6},{6,4},{5,7},{7,5},{8,10},{10,8},{9,1... | collective-permute-start | bytes 10223624 | tf_op jit(solution)/shard_map/ppermute | solution.py:603
  207.3 29.2 %collective-permute-start.7 = (f32[256,1024]{1,0:T(8,128)}, f32[256,1024]{1,0:T(8,128)S(1)}, u32[]{:S(2)}, u32[]{:S(2)}) collective-permute-start(f32[256,1024]{1,0:T(8,128)} %get-tuple-element.78.own), channel_id=1, source_target_pairs={{0,1},{1,0},{2,3},{3,2},{4,5},{5,4},{6,7},{7,6},{8,9},{9,8},{10,11... | collective-permute-start | bytes 3145736 | tf_op jit(solution)/shard_map/ppermute | solution.py:599
  209.2 27.4 %collective-permute-start.8 = (f32[256,128]{1,0:T(8,128)}, f32[256,128]{1,0:T(8,128)S(1)}, u32[]{:S(2)}, u32[]{:S(2)}) collective-permute-start(f32[256,128]{1,0:T(8,128)} %get-tuple-element.79.gate_own), channel_id=1, source_target_pairs={{0,1},{1,0},{2,3},{3,2},{4,5},{5,4},{6,7},{7,6},{8,9},{9,8},{10,11... | collective-permute-start | bytes 393224 | tf_op jit(solution)/shard_map/ppermute | solution.py:599
  209.5 49.6 %collective-permute-start.3 = (f32[256,1024]{1,0:T(8,128)S(1)}, f32[256,1024]{1,0:T(8,128)S(1)}, u32[]{:S(2)}, u32[]{:S(2)}) collective-permute-start(f32[256,1024]{1,0:T(8,128)S(1)} %copy-done.37), channel_id=1, source_target_pairs={{0,1},{1,0},{2,3},{3,2},{4,5},{5,4},{6,7},{7,6},{8,9},{9,8},{10,11... | collective-permute-start | bytes 3145736 | tf_op jit(solution)/shard_map/ppermute | solution.py:599
  252.6 23.0 %collective-permute-start.9 = (f32[256,1024]{1,0:T(8,128)}, f32[256,1024]{1,0:T(8,128)S(1)}, u32[]{:S(2)}, u32[]{:S(2)}) collective-permute-start(f32[256,1024]{1,0:T(8,128)} %get-tuple-element.87), channel_id=1, source_target_pairs={{0,1},{1,0},{2,3},{3,2},{4,5},{5,4},{6,7},{7,6},{8,9},{9,8},{10,11... | collective-permute-start | bytes 3145736 | tf_op jit(solution)/shard_map/ppermute | solution.py:599
  254.5 95.5 %collective-permute-start.65 = (f32[512,3072]{1,0:T(8,128)}, f32[512,3072]{1,0:T(8,128)S(1)}, u32[]{:S(2)}, u32[]{:S(2)}) collective-permute-start(f32[512,3072]{1,0:T(8,128)} %get-tuple-element.95), channel_id=1, source_target_pairs={{0,2},{2,0},{1,3},{3,1},{4,6},{6,4},{5,7},{7,5},{8,10},{10,8},{9,1... | collective-permute-start | bytes 18874376 | tf_op jit(solution)/shard_map/ppermute | solution.py:628
  260.0 149.3 %collective-permute-start.47 = (f32[512,3072]{1,0:T(8,128)}, f32[512,3072]{1,0:T(8,128)}, u32[]{:S(2)}, u32[]{:S(2)}) collective-permute-start(f32[512,3072]{1,0:T(8,128)} %get-tuple-element.93), channel_id=1, source_target_pairs={{0,2},{2,0},{1,3},{3,1},{4,6},{6,4},{5,7},{7,5},{8,10},{10,8},{9,1... | collective-permute-start | bytes 18874376 | tf_op jit(solution)/shard_map/ppermute | solution.py:603
  276.3 10.0 %collective-permute-start.41 = (f32[256,384]{1,0:T(8,128)S(1)}, f32[256,384]{1,0:T(8,128)S(1)}, u32[]{:S(2)}, u32[]{:S(2)}) collective-permute-start(f32[256,384]{1,0:T(8,128)S(1)} %get-tuple-element.147), channel_id=1, source_target_pairs={{0,12},{4,8},{8,4},{12,0},{1,13},{5,9},{9,5},{13,1},{2,14},{6,10},... | collective-permute-start | bytes 1179656 | tf_op jit(solution)/shard_map/ppermute | solution.py:614
  280.5 9.0 %collective-permute-start.37 = (f32[256,384]{1,0:T(8,128)S(1)}, f32[256,384]{1,0:T(8,128)S(1)}, u32[]{:S(2)}, u32[]{:S(2)}) collective-permute-start(f32[256,384]{1,0:T(8,128)S(1)} %get-tuple-element.149), channel_id=1, source_target_pairs={{0,96},{32,64},{64,32},{96,0},{1,97},{33,65},{65,33},{97,1},{2,98}... | collective-permute-start | bytes 1179656 | tf_op jit(solution)/shard_map/ppermute | solution.py:614
  283.5 7.8 %collective-permute-start.33 = (f32[256,384]{1,0:T(8,128)S(1)}, f32[256,384]{1,0:T(8,128)S(1)}, u32[]{:S(2)}, u32[]{:S(2)}) collective-permute-start(f32[256,384]{1,0:T(8,128)S(1)} %get-tuple-element.151), channel_id=1, source_target_pairs={{0,4},{4,0},{8,12},{12,8},{1,5},{5,1},{9,13},{13,9},{2,6},{6,2},{1... | collective-permute-start | bytes 1179656 | tf_op jit(solution)/shard_map/ppermute | solution.py:614
  286.3 11.3 %collective-permute-start.29 = (f32[256,512]{1,0:T(8,128)S(1)}, f32[256,512]{1,0:T(8,128)S(1)}, u32[]{:S(2)}, u32[]{:S(2)}) collective-permute-start(f32[256,512]{1,0:T(8,128)S(1)} %get-tuple-element.145), channel_id=1, source_target_pairs={{0,32},{32,0},{64,96},{96,64},{1,33},{33,1},{65,97},{97,65},{2,34}... | collective-permute-start | bytes 1572872 | tf_op jit(solution)/shard_map/ppermute | solution.py:614
  289.5 65.3 %collective-permute-start.10 = (f32[512,1664]{1,0:T(8,128)}, f32[512,1664]{1,0:T(8,128)}, u32[]{:S(2)}, u32[]{:S(2)}) collective-permute-start(f32[512,1664]{1,0:T(8,128)} %get-tuple-element.89), channel_id=1, source_target_pairs={{0,2},{2,0},{1,3},{3,1},{4,6},{6,4},{5,7},{7,5},{8,10},{10,8},{9,1... | collective-permute-start | bytes 10223624 | tf_op jit(solution)/shard_map/ppermute | solution.py:603
  291.2 9.7 %collective-permute-start.42 = (f32[128,384]{1,0:T(8,128)S(1)}, f32[128,384]{1,0:T(8,128)S(1)}, u32[]{:S(2)}, u32[]{:S(2)}) collective-permute-start(f32[128,384]{1,0:T(8,128)S(1)} %get-tuple-element.185), channel_id=1, source_target_pairs={{0,32},{32,0},{64,96},{96,64},{1,33},{33,1},{65,97},{97,65},{2,34}... | collective-permute-start | bytes 589832 | tf_op jit(solution)/shard_map/ppermute | solution.py:614
  297.6 6.9 %collective-permute-start.38 = (f32[128,384]{1,0:T(8,128)S(1)}, f32[128,384]{1,0:T(8,128)S(1)}, u32[]{:S(2)}, u32[]{:S(2)}) collective-permute-start(f32[128,384]{1,0:T(8,128)S(1)} %get-tuple-element.183), channel_id=1, source_target_pairs={{0,12},{4,8},{8,4},{12,0},{1,13},{5,9},{9,5},{13,1},{2,14},{6,10},... | collective-permute-start | bytes 589832 | tf_op jit(solution)/shard_map/ppermute | solution.py:614
  300.9 7.0 %collective-permute-start.34 = (f32[128,384]{1,0:T(8,128)S(1)}, f32[128,384]{1,0:T(8,128)S(1)}, u32[]{:S(2)}, u32[]{:S(2)}) collective-permute-start(f32[128,384]{1,0:T(8,128)S(1)} %get-tuple-element.181), channel_id=1, source_target_pairs={{0,96},{32,64},{64,32},{96,0},{1,97},{33,65},{65,33},{97,1},{2,98}... | collective-permute-start | bytes 589832 | tf_op jit(solution)/shard_map/ppermute | solution.py:614
  304.5 24.3 %collective-permute-start.30 = (f32[128,512]{1,0:T(8,128)S(1)}, f32[128,512]{1,0:T(8,128)S(1)}, u32[]{:S(2)}, u32[]{:S(2)}) collective-permute-start(f32[128,512]{1,0:T(8,128)S(1)} %get-tuple-element.169), channel_id=1, source_target_pairs={{0,4},{4,0},{8,12},{12,8},{1,5},{5,1},{9,13},{13,9},{2,6},{6,2},{1... | collective-permute-start | bytes 786440 | tf_op jit(solution)/shard_map/ppermute | solution.py:614
  317.3 5.8 collective-permute-start.35
  323.1 5.6 collective-permute-start.44
  328.7 12.5 %collective-permute-start.36 = (f32[32,384]{1,0:T(8,128)S(1)}, f32[32,384]{1,0:T(8,128)S(1)}, u32[]{:S(2)}, u32[]{:S(2)}) collective-permute-start(f32[32,384]{1,0:T(8,128)S(1)} %slice_add_fusion.91), channel_id=1, source_target_pairs={{0,32},{32,0},{64,96},{96,64},{1,33},{33,1},{65,97},{97,65},{2,34}... | collective-permute-start | bytes 147464 | tf_op jit(solution)/shard_map/ppermute | solution.py:614
  332.8 6.2 %collective-permute-start.31 = (f32[64,512]{1,0:T(8,128)S(1)}, f32[64,512]{1,0:T(8,128)S(1)}, u32[]{:S(2)}, u32[]{:S(2)}) collective-permute-start(f32[64,512]{1,0:T(8,128)S(1)} %get-tuple-element.193), channel_id=1, source_target_pairs={{0,96},{32,64},{64,32},{96,0},{1,97},{33,65},{65,33},{97,1},{2,98}... | collective-permute-start | bytes 393224 | tf_op jit(solution)/shard_map/ppermute | solution.py:614
  339.0 5.6 collective-permute-start.32
  345.3 8.4 %collective-permute-start.45 = (f32[16,1664]{1,0:T(8,128)}, f32[16,1664]{1,0:T(8,128)S(1)}, u32[]{:S(2)}, u32[]{:S(2)}) collective-permute-start(f32[16,1664]{1,0:T(8,128)} %slice.1081), channel_id=1, source_target_pairs={{0,16},{16,0},{1,17},{17,1},{2,18},{18,2},{3,19},{19,3},{4,20},{20... | collective-permute-start | bytes 319496 | tf_op jit(solution)/shard_map/ppermute | solution.py:622
  357.6 10.5 %collective-permute-start.23 = (f32[256,384]{1,0:T(8,128)S(1)}, f32[256,384]{1,0:T(8,128)S(1)}, u32[]{:S(2)}, u32[]{:S(2)}) collective-permute-start(f32[256,384]{1,0:T(8,128)S(1)} %get-tuple-element.155), channel_id=1, source_target_pairs={{0,12},{4,8},{8,4},{12,0},{1,13},{5,9},{9,5},{13,1},{2,14},{6,10},... | collective-permute-start | bytes 1179656 | tf_op jit(solution)/shard_map/ppermute | solution.py:614
  359.8 9.8 %collective-permute-start.19 = (f32[256,384]{1,0:T(8,128)S(1)}, f32[256,384]{1,0:T(8,128)S(1)}, u32[]{:S(2)}, u32[]{:S(2)}) collective-permute-start(f32[256,384]{1,0:T(8,128)S(1)} %get-tuple-element.157), channel_id=1, source_target_pairs={{0,96},{32,64},{64,32},{96,0},{1,97},{33,65},{65,33},{97,1},{2,98}... | collective-permute-start | bytes 1179656 | tf_op jit(solution)/shard_map/ppermute | solution.py:614
  362.5 9.3 %collective-permute-start.15 = (f32[256,384]{1,0:T(8,128)S(1)}, f32[256,384]{1,0:T(8,128)S(1)}, u32[]{:S(2)}, u32[]{:S(2)}) collective-permute-start(f32[256,384]{1,0:T(8,128)S(1)} %get-tuple-element.159), channel_id=1, source_target_pairs={{0,4},{4,0},{8,12},{12,8},{1,5},{5,1},{9,13},{13,9},{2,6},{6,2},{1... | collective-permute-start | bytes 1179656 | tf_op jit(solution)/shard_map/ppermute | solution.py:614
  364.0 11.0 %collective-permute-start.11 = (f32[256,512]{1,0:T(8,128)S(1)}, f32[256,512]{1,0:T(8,128)S(1)}, u32[]{:S(2)}, u32[]{:S(2)}) collective-permute-start(f32[256,512]{1,0:T(8,128)S(1)} %get-tuple-element.153), channel_id=1, source_target_pairs={{0,32},{32,0},{64,96},{96,64},{1,33},{33,1},{65,97},{97,65},{2,34}... | collective-permute-start | bytes 1572872 | tf_op jit(solution)/shard_map/ppermute | solution.py:614
  368.1 9.4 %collective-permute-start.24 = (f32[128,384]{1,0:T(8,128)S(1)}, f32[128,384]{1,0:T(8,128)S(1)}, u32[]{:S(2)}, u32[]{:S(2)}) collective-permute-start(f32[128,384]{1,0:T(8,128)S(1)} %get-tuple-element.191), channel_id=1, source_target_pairs={{0,32},{32,0},{64,96},{96,64},{1,33},{33,1},{65,97},{97,65},{2,34}... | collective-permute-start | bytes 589832 | tf_op jit(solution)/shard_map/ppermute | solution.py:614
  369.6 10.3 %collective-permute-start.20 = (f32[128,384]{1,0:T(8,128)S(1)}, f32[128,384]{1,0:T(8,128)S(1)}, u32[]{:S(2)}, u32[]{:S(2)}) collective-permute-start(f32[128,384]{1,0:T(8,128)S(1)} %get-tuple-element.189), channel_id=1, source_target_pairs={{0,12},{4,8},{8,4},{12,0},{1,13},{5,9},{9,5},{13,1},{2,14},{6,10},... | collective-permute-start | bytes 589832 | tf_op jit(solution)/shard_map/ppermute | solution.py:614
  371.8 8.3 %collective-permute-start.16 = (f32[128,384]{1,0:T(8,128)S(1)}, f32[128,384]{1,0:T(8,128)S(1)}, u32[]{:S(2)}, u32[]{:S(2)}) collective-permute-start(f32[128,384]{1,0:T(8,128)S(1)} %get-tuple-element.187), channel_id=1, source_target_pairs={{0,96},{32,64},{64,32},{96,0},{1,97},{33,65},{65,33},{97,1},{2,98}... | collective-permute-start | bytes 589832 | tf_op jit(solution)/shard_map/ppermute | solution.py:614
  375.1 14.1 %collective-permute-start.12 = (f32[128,512]{1,0:T(8,128)S(1)}, f32[128,512]{1,0:T(8,128)S(1)}, u32[]{:S(2)}, u32[]{:S(2)}) collective-permute-start(f32[128,512]{1,0:T(8,128)S(1)} %get-tuple-element.171), channel_id=1, source_target_pairs={{0,4},{4,0},{8,12},{12,8},{1,5},{5,1},{9,13},{13,9},{2,6},{6,2},{1... | collective-permute-start | bytes 786440 | tf_op jit(solution)/shard_map/ppermute | solution.py:614
  377.6 6.1 %collective-permute-start.25 = (f32[64,384]{1,0:T(8,128)S(1)}, f32[64,384]{1,0:T(8,128)S(1)}, u32[]{:S(2)}, u32[]{:S(2)}) collective-permute-start(f32[64,384]{1,0:T(8,128)S(1)} %get-tuple-element.207), channel_id=1, source_target_pairs={{0,4},{4,0},{8,12},{12,8},{1,5},{5,1},{9,13},{13,9},{2,6},{6,2},{1... | collective-permute-start | bytes 294920 | tf_op jit(solution)/shard_map/ppermute | solution.py:614
  380.0 5.0 collective-permute-start.21
  380.1 6.3 %collective-permute-start.17 = (f32[64,384]{1,0:T(8,128)S(1)}, f32[64,384]{1,0:T(8,128)S(1)}, u32[]{:S(2)}, u32[]{:S(2)}) collective-permute-start(f32[64,384]{1,0:T(8,128)S(1)} %get-tuple-element.203), channel_id=1, source_target_pairs={{0,12},{4,8},{8,4},{12,0},{1,13},{5,9},{9,5},{13,1},{2,14},{6,10},... | collective-permute-start | bytes 294920 | tf_op jit(solution)/shard_map/ppermute | solution.py:614
  383.7 5.5 collective-permute-start.26
  385.0 5.1 collective-permute-start.22
  386.4 10.5 %collective-permute-start.18 = (f32[32,384]{1,0:T(8,128)S(1)}, f32[32,384]{1,0:T(8,128)S(1)}, u32[]{:S(2)}, u32[]{:S(2)}) collective-permute-start(f32[32,384]{1,0:T(8,128)S(1)} %slice_add_fusion.97), channel_id=1, source_target_pairs={{0,32},{32,0},{64,96},{96,64},{1,33},{33,1},{65,97},{97,65},{2,34}... | collective-permute-start | bytes 147464 | tf_op jit(solution)/shard_map/ppermute | solution.py:614
  389.2 6.7 %collective-permute-start.13 = (f32[64,512]{1,0:T(8,128)S(1)}, f32[64,512]{1,0:T(8,128)S(1)}, u32[]{:S(2)}, u32[]{:S(2)}) collective-permute-start(f32[64,512]{1,0:T(8,128)S(1)} %get-tuple-element.195), channel_id=1, source_target_pairs={{0,96},{32,64},{64,32},{96,0},{1,97},{33,65},{65,33},{97,1},{2,98}... | collective-permute-start | bytes 393224 | tf_op jit(solution)/shard_map/ppermute | solution.py:614
  395.9 6.7 %collective-permute-start.14 = (f32[32,512]{1,0:T(8,128)S(1)}, f32[32,512]{1,0:T(8,128)S(1)}, u32[]{:S(2)}, u32[]{:S(2)}) collective-permute-start(f32[32,512]{1,0:T(8,128)S(1)} %slice_add_fusion.85), channel_id=1, source_target_pairs={{0,12},{4,8},{8,4},{12,0},{1,13},{5,9},{9,5},{13,1},{2,14},{6,10},... | collective-permute-start | bytes 196616 | tf_op jit(solution)/shard_map/ppermute | solution.py:614
  402.6 6.6 %collective-permute-start.27 = (f32[16,1664]{1,0:T(8,128)S(1)}, f32[16,1664]{1,0:T(8,128)S(1)}, u32[]{:S(2)}, u32[]{:S(2)}) collective-permute-start(f32[16,1664]{1,0:T(8,128)S(1)} %slice.1022), channel_id=1, source_target_pairs={{0,16},{16,0},{1,17},{17,1},{2,18},{18,2},{3,19},{19,3},{4,20},{20... | collective-permute-start | bytes 319496 | tf_op jit(solution)/shard_map/ppermute | solution.py:622
  413.2 19.2 %collective-permute-start.60 = (f32[256,768]{1,0:T(8,128)S(1)}, f32[256,768]{1,0:T(8,128)S(1)}, u32[]{:S(2)}, u32[]{:S(2)}) collective-permute-start(f32[256,768]{1,0:T(8,128)S(1)} %get-tuple-element.137), channel_id=1, source_target_pairs={{0,12},{4,8},{8,4},{12,0},{1,13},{5,9},{9,5},{13,1},{2,14},{6,10},... | collective-permute-start | bytes 2359304 | tf_op jit(solution)/shard_map/ppermute | solution.py:614
  414.7 49.3 %collective-permute-start.46 = (f32[2,16]{1,0:T(2,128)S(1)}, f32[2,16]{1,0:T(2,128)S(1)}, u32[]{:S(2)}, u32[]{:S(2)}) collective-permute-start(f32[2,16]{1,0:T(2,128)S(1)} %get-tuple-element.135), channel_id=1, source_target_pairs={{0,1},{1,0},{2,3},{3,2},{4,5},{5,4},{6,7},{7,6},{8,9},{9,8},{10,11... | collective-permute-start | bytes 392 | tf_op jit(solution)/shard_map/ppermute | solution.py:599
  415.7 16.8 %collective-permute-start.56 = (f32[256,768]{1,0:T(8,128)S(1)}, f32[256,768]{1,0:T(8,128)S(1)}, u32[]{:S(2)}, u32[]{:S(2)}) collective-permute-start(f32[256,768]{1,0:T(8,128)S(1)} %get-tuple-element.139), channel_id=1, source_target_pairs={{0,96},{32,64},{64,32},{96,0},{1,97},{33,65},{65,33},{97,1},{2,98}... | collective-permute-start | bytes 2359304 | tf_op jit(solution)/shard_map/ppermute | solution.py:614
  415.7 20.0 %collective-permute-start.52 = (f32[256,768]{1,0:T(8,128)S(1)}, f32[256,768]{1,0:T(8,128)S(1)}, u32[]{:S(2)}, u32[]{:S(2)}) collective-permute-start(f32[256,768]{1,0:T(8,128)S(1)} %get-tuple-element.141), channel_id=1, source_target_pairs={{0,4},{4,0},{8,12},{12,8},{1,5},{5,1},{9,13},{13,9},{2,6},{6,2},{1... | collective-permute-start | bytes 2359304 | tf_op jit(solution)/shard_map/ppermute | solution.py:614
  416.6 21.0 %collective-permute-start.48 = (f32[256,768]{1,0:T(8,128)S(1)}, f32[256,768]{1,0:T(8,128)S(1)}, u32[]{:S(2)}, u32[]{:S(2)}) collective-permute-start(f32[256,768]{1,0:T(8,128)S(1)} %get-tuple-element.143), channel_id=1, source_target_pairs={{0,32},{32,0},{64,96},{96,64},{1,33},{33,1},{65,97},{97,65},{2,34}... | collective-permute-start | bytes 2359304 | tf_op jit(solution)/shard_map/ppermute | solution.py:614
  432.4 10.1 %collective-permute-start.61 = (f32[128,768]{1,0:T(8,128)S(1)}, f32[128,768]{1,0:T(8,128)S(1)}, u32[]{:S(2)}, u32[]{:S(2)}) collective-permute-start(f32[128,768]{1,0:T(8,128)S(1)} %get-tuple-element.167), channel_id=1, source_target_pairs={{0,32},{32,0},{64,96},{96,64},{1,33},{33,1},{65,97},{97,65},{2,34}... | collective-permute-start | bytes 1179656 | tf_op jit(solution)/shard_map/ppermute | solution.py:614
  432.7 11.3 %collective-permute-start.57 = (f32[128,768]{1,0:T(8,128)S(1)}, f32[128,768]{1,0:T(8,128)S(1)}, u32[]{:S(2)}, u32[]{:S(2)}) collective-permute-start(f32[128,768]{1,0:T(8,128)S(1)} %get-tuple-element.165), channel_id=1, source_target_pairs={{0,12},{4,8},{8,4},{12,0},{1,13},{5,9},{9,5},{13,1},{2,14},{6,10},... | collective-permute-start | bytes 1179656 | tf_op jit(solution)/shard_map/ppermute | solution.py:614
  435.9 10.2 %collective-permute-start.53 = (f32[128,768]{1,0:T(8,128)S(1)}, f32[128,768]{1,0:T(8,128)S(1)}, u32[]{:S(2)}, u32[]{:S(2)}) collective-permute-start(f32[128,768]{1,0:T(8,128)S(1)} %get-tuple-element.163), channel_id=1, source_target_pairs={{0,96},{32,64},{64,32},{96,0},{1,97},{33,65},{65,33},{97,1},{2,98}... | collective-permute-start | bytes 1179656 | tf_op jit(solution)/shard_map/ppermute | solution.py:614
  437.7 9.1 %collective-permute-start.49 = (f32[128,768]{1,0:T(8,128)S(1)}, f32[128,768]{1,0:T(8,128)S(1)}, u32[]{:S(2)}, u32[]{:S(2)}) collective-permute-start(f32[128,768]{1,0:T(8,128)S(1)} %get-tuple-element.161), channel_id=1, source_target_pairs={{0,4},{4,0},{8,12},{12,8},{1,5},{5,1},{9,13},{13,9},{2,6},{6,2},{1... | collective-permute-start | bytes 1179656 | tf_op jit(solution)/shard_map/ppermute | solution.py:614
  442.5 7.5 %collective-permute-start.62 = (f32[64,768]{1,0:T(8,128)S(1)}, f32[64,768]{1,0:T(8,128)S(1)}, u32[]{:S(2)}, u32[]{:S(2)}) collective-permute-start(f32[64,768]{1,0:T(8,128)S(1)} %get-tuple-element.179), channel_id=1, source_target_pairs={{0,4},{4,0},{8,12},{12,8},{1,5},{5,1},{9,13},{13,9},{2,6},{6,2},{1... | collective-permute-start | bytes 589832 | tf_op jit(solution)/shard_map/ppermute | solution.py:614
  444.1 6.6 %collective-permute-start.58 = (f32[64,768]{1,0:T(8,128)S(1)}, f32[64,768]{1,0:T(8,128)S(1)}, u32[]{:S(2)}, u32[]{:S(2)}) collective-permute-start(f32[64,768]{1,0:T(8,128)S(1)} %get-tuple-element.177), channel_id=1, source_target_pairs={{0,32},{32,0},{64,96},{96,64},{1,33},{33,1},{65,97},{97,65},{2,34}... | collective-permute-start | bytes 589832 | tf_op jit(solution)/shard_map/ppermute | solution.py:614
  446.1 7.1 %collective-permute-start.54 = (f32[64,768]{1,0:T(8,128)S(1)}, f32[64,768]{1,0:T(8,128)S(1)}, u32[]{:S(2)}, u32[]{:S(2)}) collective-permute-start(f32[64,768]{1,0:T(8,128)S(1)} %get-tuple-element.175), channel_id=1, source_target_pairs={{0,12},{4,8},{8,4},{12,0},{1,13},{5,9},{9,5},{13,1},{2,14},{6,10},... | collective-permute-start | bytes 589832 | tf_op jit(solution)/shard_map/ppermute | solution.py:614
  446.9 7.1 %collective-permute-start.50 = (f32[64,768]{1,0:T(8,128)S(1)}, f32[64,768]{1,0:T(8,128)S(1)}, u32[]{:S(2)}, u32[]{:S(2)}) collective-permute-start(f32[64,768]{1,0:T(8,128)S(1)} %get-tuple-element.173), channel_id=1, source_target_pairs={{0,96},{32,64},{64,32},{96,0},{1,97},{33,65},{65,33},{97,1},{2,98}... | collective-permute-start | bytes 589832 | tf_op jit(solution)/shard_map/ppermute | solution.py:614
  450.0 6.8 %collective-permute-start.63 = (f32[32,768]{1,0:T(8,128)S(1)}, f32[32,768]{1,0:T(8,128)S(1)}, u32[]{:S(2)}, u32[]{:S(2)}) collective-permute-start(f32[32,768]{1,0:T(8,128)S(1)} %slice_add_fusion.63), channel_id=1, source_target_pairs={{0,96},{32,64},{64,32},{96,0},{1,97},{33,65},{65,33},{97,1},{2,98}... | collective-permute-start | bytes 294920 | tf_op jit(solution)/shard_map/ppermute | solution.py:614
  450.6 6.2 %collective-permute-start.59 = (f32[32,768]{1,0:T(8,128)S(1)}, f32[32,768]{1,0:T(8,128)S(1)}, u32[]{:S(2)}, u32[]{:S(2)}) collective-permute-start(f32[32,768]{1,0:T(8,128)S(1)} %slice_add_fusion.65), channel_id=1, source_target_pairs={{0,4},{4,0},{8,12},{12,8},{1,5},{5,1},{9,13},{13,9},{2,6},{6,2},{1... | collective-permute-start | bytes 294920 | tf_op jit(solution)/shard_map/ppermute | solution.py:614
  453.3 4.9 collective-permute-start.55
  454.1 6.0 %collective-permute-start.51 = (f32[32,768]{1,0:T(8,128)S(1)}, f32[32,768]{1,0:T(8,128)S(1)}, u32[]{:S(2)}, u32[]{:S(2)}) collective-permute-start(f32[32,768]{1,0:T(8,128)S(1)} %slice_add_fusion.69), channel_id=1, source_target_pairs={{0,12},{4,8},{8,4},{12,0},{1,13},{5,9},{9,5},{13,1},{2,14},{6,10},... | collective-permute-start | bytes 294920 | tf_op jit(solution)/shard_map/ppermute | solution.py:614
  460.2 7.4 %collective-permute-start.64 = (f32[16,3072]{1,0:T(8,128)S(1)}, f32[16,3072]{1,0:T(8,128)S(1)}, u32[]{:S(2)}, u32[]{:S(2)}) collective-permute-start(f32[16,3072]{1,0:T(8,128)S(1)} %slice.1152), channel_id=1, source_target_pairs={{0,16},{16,0},{1,17},{17,1},{2,18},{18,2},{3,19},{19,3},{4,20},{20... | collective-permute-start | bytes 589832 | tf_op jit(solution)/shard_map/ppermute | solution.py:622
  (58 other events, 920.3 us)
Sparse Core Ops, SparseCore 0:
  353.9 234.7 reduce-scatter.1
